TPU v7x, 32 devices: a whole 2x2x4 slice. The times are simulated.
32 devices in a mesh: lat: 8 (over z, y), lon: 4 (over x, core).
Axes of the slice: x: 2, y: 2, z: 4, core: 2. Of those that a mesh axis runs over, the one named last changes fastest.
Arguments:
- views: bfloat16 [2, 32, 192, 4096], P(None, 'lat', None, 'lon'), may hold values from -8 to 8
- conv_weight: bfloat16 [9, 192, 192], replicated, may hold values from -0.15625 to 0.15625
- match_weight: bfloat16 [128, 192], replicated, may hold values from -0.4375 to 0.4375
- value_weight: bfloat16 [128, 192], replicated, may hold values from -0.4375 to 0.4375
- post_gain: float32 [128], replicated, may hold values from 0.1 to 1.9
- out_weight: bfloat16 [192, 128], replicated, may hold values from -0.5 to 0.5
Outputs:
- coded_maps: bfloat16 [2, 32, 192, 4096], P(None, 'lat', None, 'lon')
All inputs are finite; a program needn't handle non-finite values.
Results may differ from a plain program's by a relative error of at most 0.0054.
Values may be sent and summed in bfloat16 or wider, within the bound.
A program may use at most 320 MiB of HBM per device.

v0:
```python
import jax
import jax.numpy as jnp
from jax import lax
from jax.sharding import PartitionSpec as P


def with_halo(cells, sides, width, closed):
    for axis, dim in sides:
        count = lax.axis_size(axis)
        ends = count if closed else count - 1
        head = lax.slice_in_dim(cells, 0, width, axis=dim)
        tail = lax.slice_in_dim(cells, cells.shape[dim] - width, cells.shape[dim], axis=dim)
        cells = jnp.concatenate(
            [
                lax.ppermute(tail, axis, [(i, (i + 1) % count) for i in range(ends)]),
                cells,
                lax.ppermute(head, axis, [((i + 1) % count, i) for i in range(ends)]),
            ],
            axis=dim,
        )
    return cells


def attend(state_now, key_rows, value_rows, queries, score_scale):
    running_max, running_sum, numerator = state_now
    key_count = key_rows.shape[-1]
    for offset in range(0, key_count, 1024):
        block_len = min(1024, key_count - offset)
        key_block = key_rows[..., offset : offset + block_len]
        value_block = value_rows[..., offset : offset + block_len]
        scores = (
            jnp.einsum("vrai,vraj->vrij", queries, key_block, preferred_element_type=jnp.float32)
            * score_scale
        )
        new_max = jnp.maximum(running_max, jnp.max(scores, axis=-1))
        weights = jnp.exp(scores - new_max[..., None])
        factor = jnp.exp(running_max - new_max)
        running_sum = running_sum * factor + jnp.sum(weights, axis=-1)
        numerator = numerator * factor[:, :, None, :] + jnp.einsum(
            "vrij,vraj->vrai",
            weights.astype(jnp.bfloat16),
            value_block,
            preferred_element_type=jnp.float32,
        )
        running_max = new_max
    return (running_max, running_sum, numerator)


def start_state(row_count, channels, query_count):
    return (
        jnp.full((2, row_count, query_count), -1e30, jnp.float32),
        jnp.zeros((2, row_count, query_count), jnp.float32),
        jnp.zeros((2, row_count, channels, query_count), jnp.float32),
    )


def finish(running_sum, numerator, post_gain):
    attended = numerator / running_sum[:, :, None, :]
    normed = (
        attended
        * lax.rsqrt(jnp.mean(attended * attended, axis=2, keepdims=True) + 1e-06)
        * post_gain[None, None, :, None]
    )
    return normed.astype(jnp.bfloat16)


def body(views, conv_weight, match_weight, value_weight, post_gain, out_weight):
    row_count = views.shape[1]
    col_count = views.shape[3]
    channels = match_weight.shape[0]
    with_rows = with_halo(views, (("lat", 1),), 1, False)
    padded = with_halo(with_rows, (("lon", 3),), 1, True)
    center = jnp.zeros((2, row_count, conv_weight.shape[1], col_count), jnp.float32)
    side_sum = jnp.zeros((2, row_count, conv_weight.shape[1], col_count), jnp.float32)
    for row_step in range(3):
        for col_step in range(3):
            window = padded[:, row_step : row_step + row_count, :, col_step : col_step + col_count]
            term = jnp.einsum(
                "oc,vrcw->vrow",
                conv_weight[3 * row_step + col_step],
                window,
                preferred_element_type=jnp.float32,
            )
            if col_step == 1:
                center = center + term
            else:
                side_sum = side_sum + term
    row_total = row_count * lax.axis_size("lat")
    row_index = (lax.axis_index("lat") * row_count + jnp.arange(row_count, dtype=jnp.int32)).astype(
        jnp.float32
    )
    latitude = (row_index + 0.5 - 0.5 * row_total) * (2.8 / row_total)
    side_weight = 1.0 / (jnp.cos(latitude) + 0.25)
    convolved = center + side_weight[None, :, None, None] * side_sum
    refined = (views.astype(jnp.float32) + jax.nn.gelu(convolved, approximate=True)).astype(
        jnp.bfloat16
    )
    matched = jnp.einsum(
        "ac,vrcw->vraw", match_weight, refined, preferred_element_type=jnp.float32
    ).astype(jnp.bfloat16)
    valued = jnp.einsum(
        "ac,vrcw->vraw", value_weight, refined, preferred_element_type=jnp.float32
    ).astype(jnp.bfloat16)
    score_scale = 1.0 / channels**0.5
    initial = start_state(row_count, channels, col_count)
    running_max, running_sum, numerator = attend(
        initial,
        jnp.flip(lax.all_gather(matched, "lon", axis=3, tiled=True), 0),
        jnp.flip(lax.all_gather(valued, "lon", axis=3, tiled=True), 0),
        matched,
        score_scale,
    )
    normed = finish(running_sum, numerator, post_gain)
    delta = jnp.einsum("ca,vraw->vrcw", out_weight, normed, preferred_element_type=jnp.float32)
    return (refined.astype(jnp.float32) + delta).astype(jnp.bfloat16)


def solution(mesh):
    placed = (P(None, "lat", None, "lon"), P(), P(), P(), P(), P())
    return jax.shard_map(
        body, mesh=mesh, in_specs=placed, out_specs=P(None, "lat", None, "lon"), check_vma=False
    )
```

profile of v0, /device:TPU:0, one launch (start us, length us, event | category | flops | bytes accessed | tf_op | source)
XLA Modules:
  0.0 420.5 jit_solution(14702197791458834470)
XLA Ops:
  6.5 2.8 fusion.105
  9.3 5.8 %collective-permute-start = (bf16[2,1,192,1024]{3,2,1,0:T(8,128)(2,1)}, bf16[2,1,192,1024]{3,2,1,0:T(8,128)(2,1)}, u32[]{:S(2)}, u32[]{:S(2)}) collective-permute-start(bf16[2,1,192,1024]{3,2,1,0:T(8,128)(2,1)} %get-tuple-element.19), channel_id=1, source_target_pairs={{0,4},{4,8},{8,12},{12,16},{16,20},{20,24},{24,28},{1,5},{5,9},{9,... | collective-permute-start | bytes 2359304 | tf_op jit(solution)/shard_map/ppermute | solution.py:15
  16.4 4.5 %fusion.73 = f32[2,4,1024,192]{2,3,1,0:T(8,128)} fusion(bf16[2,4,192,1024]{3,2,1,0:T(8,128)(2,1)S(1)} %copy-done.3, bf16[9,192,192]{2,1,0:T(8,128)(2,1)} %param.7), kind=kOutput, calls=%fused_computation.90 | convolution fusion | flops 603979776 | bytes 9535488 | tf_op jit(solution)/shard_map/oc,vrcw->vrow/dot_general | solution.py:78
  21.0 27.2 %collective-permute-done = bf16[2,1,192,1024]{3,2,1,0:T(8,128)(2,1)} collective-permute-done((bf16[2,1,192,1024]{3,2,1,0:T(8,128)(2,1)}, bf16[2,1,192,1024]{3,2,1,0:T(8,128)(2,1)}, u32[]{:S(2)}, u32[]{:S(2)}) %collective-permute-start) | collective-permute-done | bytes 786464 | tf_op jit(solution)/shard_map/ppermute | solution.py:15
  58.0 4.8 %fusion.50 = f32[2,4,1024,192]{2,3,1,0:T(8,128)} fusion(bf16[2,1,192,1024]{3,2,1,0:T(8,128)(2,1)} %collective-permute-done.1, bf16[2,4,192,1024]{3,2,1,0:T(8,128)(2,1)S(1)} %copy-done.3, bf16[9,192,192]{2,1,0:T(8,128)(2,1)} %param.7), kind=kOutput, calls=%fused_computation.66 | convolution fusion | flops 610271232 | bytes 10321920 | tf_op jit(solution)/shard_map/oc,vrcw->vrow/dot_general | solution.py:78
  62.8 4.8 %fusion.52 = f32[2,4,1024,192]{2,3,1,0:T(8,128)} fusion(bf16[2,4,192,1024]{3,2,1,0:T(8,128)(2,1)S(1)} %copy-done.3, bf16[2,1,192,1024]{3,2,1,0:T(8,128)(2,1)} %collective-permute-done, bf16[9,192,192]{2,1,0:T(8,128)(2,1)} %param.7), kind=kOutput, calls=%fused_computation.69 | convolution fusion | flops 610271232 | bytes 10321920 | tf_op jit(solution)/shard_map/oc,vrcw->vrow/dot_general | solution.py:78
  68.0 6.0 %fusion.44 = f32[2,4,1024,192]{2,3,1,0:T(8,128)} fusion(bf16[2,6,192,1024]{3,2,1,0:T(8,128)(2,1)} %copy-done.2, bf16[2,6,192,1]{3,2,1,0:T(8,128)(2,1)S(1)} %copy.16, bf16[9,192,192]{2,1,0:T(8,128)(2,1)} %param.7), kind=kOutput, calls=%fused_computation.58 | convolution fusion | flops 610271232 | bytes 11112960 | tf_op jit(solution)/shard_map/oc,vrcw->vrow/dot_general | solution.py:78
  74.0 3.3 fusion.41
  77.7 6.1 %fusion.38 = f32[2,4,1024,192]{2,3,1,0:T(8,128)} fusion(bf16[2,6,192,1024]{3,2,1,0:T(8,128)(2,1)} %copy-done.2, bf16[2,6,192,1]{3,2,1,0:T(8,128)(2,1)S(1)} %copy.18, bf16[9,192,192]{2,1,0:T(8,128)(2,1)S(1)} %copy-done.10), kind=kOutput, calls=%fused_computation.54 | convolution fusion | flops 610271232 | bytes 11698176 | tf_op jit(solution)/shard_map/oc,vrcw->vrow/dot_general | solution.py:78
  83.8 3.9 fusion.35
  87.7 3.8 fusion.48
  91.6 19.7 %fusion.32 = bf16[2,4,192,1024]{3,2,1,0:T(8,128)(2,1)} fusion(f32[2,4,1024,192]{2,3,1,0:T(8,128)} %fusion.48, f32[2,4,1024,192]{2,3,1,0:T(8,128)} %fusion.35, f32[2,4,1024,192]{2,3,1,0:T(8,128)} %fusion.41, f32[2,4,1024,192]{2,3,1,0:T(8,128)} %fusion.44, f32[2,4,1024,192]{2,3,1,0:T(8,128)} %fusion.38, f32[2,4,1024,192]{2,3,1,0:T(8,128)} %fusion.50, ...), kind=kOutput, calls=%fused_computation.41 | convolution fusion | flops 641728512 | bytes 62030336 | tf_op jit(solution)/shard_map/oc,vrcw->vrow/dot_general | solution.py:78
  111.3 4.7 %convert_bitcast_fusion = bf16[2,4,128,1024]{2,3,1,0:T(8,128)(2,1)} fusion(bf16[2,4,192,1024]{3,2,1,0:T(8,128)(2,1)} %fusion.32, bf16[128,192]{0,1:T(8,128)(2,1)S(1)} %copy-done.11), kind=kOutput, calls=%fused_computation.81 | convolution fusion | flops 403701760 | bytes 5292032 | tf_op jit(solution)/shard_map/ac,vrcw->vraw/dot_general | solution.py:101
  116.3 2.7 convolution_convert_fusion
  119.1 56.7 %all-gather.5.cloned.1.call-done = bf16[2,4,128,4096]{2,3,1,0:T(8,128)(2,1)} async-done(((bf16[2,4,128,1024]{2,3,1,0:T(8,128)(2,1)}), bf16[2,4,128,4096]{2,3,1,0:T(8,128)(2,1)}) %all-gather.5.cloned.1.call-update) | async-done | bytes 8388624 | tf_op jit(solution)/shard_map/all_gather | solution.py:109
  175.8 6.0 %fusion.103 = (bf16[2,4,128,1024]{2,3,1,0:T(8,128)(2,1)}, bf16[2,4,128,1024]{2,3,1,0:T(8,128)(2,1)}, bf16[2,4,128,1024]{2,3,1,0:T(8,128)(2,1)}, bf16[2,4,128,1024]{2,3,1,0:T(8,128)(2,1)}) fusion(bf16[2,4,128,4096]{2,3,1,0:T(8,128)(2,1)} %all-gather.5.cloned.1.call-done), kind=kLoop, calls=%fused_computation.130 | loop fusion | bytes 16777216 | tf_op jit(solution)/shard_map/slice | solution.py:30
  181.9 3.4 slice.147
  185.2 3.4 slice.151
  188.7 3.6 slice.155
  192.3 43.4 %all-gather.3.cloned.1.call-done = bf16[2,4,128,4096]{2,3,1,0:T(8,128)(2,1)} async-done(((bf16[2,4,128,1024]{2,3,1,0:T(8,128)(2,1)}), bf16[2,4,128,4096]{2,3,1,0:T(8,128)(2,1)}) %all-gather.3.cloned.1.call-update) | async-done | bytes 8388624 | tf_op jit(solution)/shard_map/all_gather | solution.py:108
  235.7 14.8 %multiply_reduce_fusion.3 = (f32[2,4,1024]{2,1,0:T(4,128)S(1)}, f32[2,4,1024,1024]{2,3,1,0:T(8,128)}) fusion(bf16[2,4,1024,128]{3,2,1,0:T(8,128)(2,1)S(1)} %copy-done.1, bf16[2,4,128,4096]{2,3,1,0:T(8,128)(2,1)} %all-gather.3.cloned.1.call-done), kind=kOutput, calls=%fused_computation.7 | convolution fusion | flops 2164252672 | bytes 37781504 | tf_op jit(solution)/shard_map/vrai,vraj->vrij/dot_general | solution.py:32
  250.5 14.8 %multiply_reduce_fusion.2 = (f32[2,4,1024]{2,1,0:T(4,128)S(1)}, f32[2,4,1024,1024]{2,3,1,0:T(8,128)}) fusion(bf16[2,4,1024,128]{3,2,1,0:T(8,128)(2,1)S(1)} %copy-done.1, bf16[2,4,128,4096]{2,3,1,0:T(8,128)(2,1)} %all-gather.3.cloned.1.call-done), kind=kOutput, calls=%fused_computation.6 | convolution fusion | flops 2164252672 | bytes 37781504 | tf_op jit(solution)/shard_map/vrai,vraj->vrij/dot_general | solution.py:32
  265.3 14.8 %multiply_reduce_fusion = (f32[2,4,1024]{2,1,0:T(4,128)S(1)}, f32[2,4,1024,1024]{2,3,1,0:T(8,128)}) fusion(bf16[2,4,1024,128]{3,2,1,0:T(8,128)(2,1)S(1)} %copy-done.1, bf16[2,4,128,4096]{2,3,1,0:T(8,128)(2,1)} %all-gather.3.cloned.1.call-done), kind=kOutput, calls=%fused_computation.4 | convolution fusion | flops 2164252672 | bytes 37781504 | tf_op jit(solution)/shard_map/vrai,vraj->vrij/dot_general | solution.py:32
  280.0 14.7 %multiply_reduce_fusion.1 = (f32[2,4,1024]{2,1,0:T(4,128)S(1)}, f32[2,4,1024,1024]{2,3,1,0:T(8,128)}) fusion(bf16[2,4,1024,128]{3,2,1,0:T(8,128)(2,1)S(1)} %copy-done.1, bf16[2,4,128,4096]{2,3,1,0:T(8,128)(2,1)} %all-gather.3.cloned.1.call-done), kind=kOutput, calls=%fused_computation.5 | convolution fusion | flops 2164252672 | bytes 37781504 | tf_op jit(solution)/shard_map/vrai,vraj->vrij/dot_general | solution.py:32
  294.8 16.7 %fusion.10 = f32[2,4,128,1024]{3,2,1,0:T(8,128)} fusion(bf16[2,4,128,1024]{2,3,1,0:T(8,128)(2,1)} %slice.151, f32[2,4,1024,1024]{2,3,1,0:T(8,128)} %get-tuple-element.25, f32[2,4,1024]{2,1,0:T(4,128)S(1)} %get-tuple-element.10), kind=kOutput, calls=%fused_computation.17 | convolution fusion | flops 2172649472 | bytes 39878656 | tf_op jit(solution)/shard_map/vrij,vraj->vrai/dot_general | solution.py:39
  311.5 22.6 %fusion.4 = (f32[2,4,1024]{2,1,0:T(4,128)S(1)}, f32[2,4,1024]{2,1,0:T(4,128)S(1)}) fusion(f32[2,4,1024,1024]{2,3,1,0:T(8,128)} %get-tuple-element.25, f32[2,4,1024]{2,1,0:T(4,128)S(1)} %get-tuple-element.10, f32[2,4,1024]{2,1,0:T(4,128)S(1)} %get-tuple-element.9, f32[2,4,1024,1024]{2,3,1,0:T(8,128)} %get-tuple-element.23), kind=kLoop, calls=%fused_computation.12 | loop fusion | flops 50315264 | bytes 67239936 | tf_op jit(solution)/shard_map/reduce_sum | solution.py:38
  334.1 15.7 %fusion.8 = f32[2,4,128,1024]{3,2,1,0:T(8,128)} fusion(bf16[2,4,128,1024]{2,3,1,0:T(8,128)(2,1)S(1)} %copy-done.7, f32[2,4,1024,1024]{2,3,1,0:T(8,128)} %get-tuple-element.23, f32[2,4,1024]{2,1,0:T(4,128)S(1)} %get-tuple-element.9), kind=kOutput, calls=%fused_computation.16 | convolution fusion | flops 2172649472 | bytes 39878656 | tf_op jit(solution)/shard_map/vrij,vraj->vrai/dot_general | solution.py:39
  349.8 3.2 slice.143
  353.1 15.8 %fusion.12 = f32[2,4,128,1024]{3,2,1,0:T(8,128)} fusion(bf16[2,4,128,1024]{2,3,1,0:T(8,128)(2,1)S(1)} %copy-done.6, f32[2,4,1024,1024]{2,3,1,0:T(8,128)} %get-tuple-element.27, f32[2,4,1024]{2,1,0:T(4,128)S(1)} %get-tuple-element.11), kind=kOutput, calls=%fused_computation.18 | convolution fusion | flops 2172649472 | bytes 39878656 | tf_op jit(solution)/shard_map/vrij,vraj->vrai/dot_general | solution.py:39
  368.8 24.8 %fusion = (f32[2,4,1024]{2,1,0:T(4,128)S(1)}, f32[2,4,1024]{2,1,0:T(4,128)S(1)}) fusion(f32[2,4,1024,1024]{2,3,1,0:T(8,128)} %get-tuple-element.29, f32[2,4,1024]{2,1,0:T(4,128)S(1)} %get-tuple-element.21, f32[2,4,1024]{2,1,0:T(4,128)S(1)} %get-tuple-element.11, f32[2,4,1024,1024]{2,3,1,0:T(8,128)} %get-tuple-element.27), kind=kLoop, calls=%fused_computation.8 | loop fusion | flops 50315264 | bytes 67239936 | tf_op jit(solution)/shard_map/reduce_sum | solution.py:38
  393.8 16.7 %multiply_reduce_fusion.4 = (f32[2,4,1024]{2,1,0:T(4,128)S(1)}, f32[2,4,128,1024]{3,2,1,0:T(8,128)S(1)}) fusion(f32[2,4,1024]{2,1,0:T(4,128)S(1)} %get-tuple-element.5, f32[2,4,128,1024]{3,2,1,0:T(8,128)S(1)} %copy-done.9, f32[2,4,1024]{2,1,0:T(4,128)S(1)} %get-tuple-element.8, f32[2,4,128,1024]{3,2,1,0:T(8,128)S(1)} %copy-done.8, ...), kind=kOutput, calls=%fused_computation.49 | convolution fusion | flops 2183127040 | bytes 52658176 | tf_op jit(solution)/shard_map/vrij,vraj->vrai/dot_general | solution.py:39
  410.5 2.9 fusion.33
  (60 shorter events, 12.4 us)
Async XLA Ops:
  6.5 404.0 %copy-start = (bf16[192,128]{1,0:T(8,128)(2,1)S(1)}, bf16[192,128]{1,0:T(8,128)(2,1)}, u32[]{:S(2)}) copy-start(bf16[192,128]{1,0:T(8,128)(2,1)} %param.11) | copy-start | bytes 147460
  6.5 9.9 %copy-start.3 = (bf16[2,4,192,1024]{3,2,1,0:T(8,128)(2,1)S(1)}, bf16[2,4,192,1024]{3,2,1,0:T(8,128)(2,1)}, u32[]{:S(2)}) copy-start(bf16[2,4,192,1024]{3,2,1,0:T(8,128)(2,1)} %param.6) | copy-start | bytes 9437188
  6.5 169.3 %all-gather.5.cloned.1.call-start = ((), (), s32[]{:S(2)}) async-start(), calls=%async_computation.1 | async-start | bytes 10485760 | tf_op jit(solution)/shard_map/all_gather | solution.py:109
  9.3 38.8 %collective-permute-start = (bf16[2,1,192,1024]{3,2,1,0:T(8,128)(2,1)}, bf16[2,1,192,1024]{3,2,1,0:T(8,128)(2,1)}, u32[]{:S(2)}, u32[]{:S(2)}) collective-permute-start(bf16[2,1,192,1024]{3,2,1,0:T(8,128)(2,1)} %get-tuple-element.19), channel_id=1, source_target_pairs={{0,4},{4,8},{8,12},{12,16},{16,20},{20,24},{24,28},{1,5},{5,9},{9,... | collective-permute-start | bytes 2359304 | tf_op jit(solution)/shard_map/ppermute | solution.py:15
  15.1 34.8 %collective-permute-start.1 = (bf16[2,1,192,1024]{3,2,1,0:T(8,128)(2,1)}, bf16[2,1,192,1024]{3,2,1,0:T(8,128)(2,1)}, u32[]{:S(2)}, u32[]{:S(2)}) collective-permute-start(bf16[2,1,192,1024]{3,2,1,0:T(8,128)(2,1)} %get-tuple-element.18), channel_id=1, source_target_pairs={{4,0},{8,4},{12,8},{16,12},{20,16},{24,20},{28,24},{5,1},{9,5},{13... | collective-permute-start | bytes 2359304 | tf_op jit(solution)/shard_map/ppermute | solution.py:17
  51.1 2.2 copy-start.2
  55.9 21.4 %collective-permute-start.3 = (bf16[2,6,192,1]{2,0,3,1:T(2,128)(2,1)S(1)}, bf16[2,6,192,1]{2,0,3,1:T(2,128)(2,1)S(1)}, u32[]{:S(2)}, u32[]{:S(2)}) collective-permute-start(bf16[2,6,192,1]{2,0,3,1:T(2,128)(2,1)S(1)} %copy.17), channel_id=1, source_target_pairs={{1,0},{2,1},{3,2},{0,3},{5,4},{6,5},{7,6},{4,7},{9,8},{10,9},{11,1... | collective-permute-start | bytes 13832 | tf_op jit(solution)/shard_map/ppermute | solution.py:17
  57.4 10.2 %collective-permute-start.2 = (bf16[2,6,192,1]{2,0,3,1:T(2,128)(2,1)S(1)}, bf16[2,6,192,1]{2,0,3,1:T(2,128)(2,1)S(1)}, u32[]{:S(2)}, u32[]{:S(2)}) collective-permute-start(bf16[2,6,192,1]{2,0,3,1:T(2,128)(2,1)S(1)} %copy.15), channel_id=1, source_target_pairs={{0,1},{1,2},{2,3},{3,0},{4,5},{5,6},{6,7},{7,4},{8,9},{9,10},{10,1... | collective-permute-start | bytes 13832 | tf_op jit(solution)/shard_map/ppermute | solution.py:15
  67.6 6.4 %slice-start = ((s8[4718592]{0:T(1024)(128)(4,1)}), s8[524288]{0:T(1024)(128)(4,1)S(1)}, s32[]{:S(2)}) async-start(s8[4718592]{0:T(1024)(128)(4,1)} %bitcast.99), calls=%async_computation.2 | async-start | bytes 1048576
  67.9 6.0 %slice-start.1 = ((s8[4718592]{0:T(1024)(128)(4,1)}), s8[4194304]{0:T(1024)(128)(4,1)S(1)}, s32[]{:S(2)}) async-start(s8[4718592]{0:T(1024)(128)(4,1)} %bitcast.99), calls=%async_computation.3 | async-start | bytes 8388608
  68.0 6.0 %copy-start.10 = (bf16[9,192,192]{2,1,0:T(8,128)(2,1)S(1)}, bf16[9,192,192]{2,1,0:T(8,128)(2,1)}, u32[]{:S(2)}) copy-start(bf16[9,192,192]{2,1,0:T(8,128)(2,1)} %param.7) | copy-start | bytes 1990660
  77.3 6.5 %slice-start.2 = ((s8[4718592]{0:T(1024)(128)(4,1)}), s8[524288]{0:T(1024)(128)(4,1)S(1)}, s32[]{:S(2)}) async-start(s8[4718592]{0:T(1024)(128)(4,1)} %bitcast.101), calls=%async_computation.4 | async-start | bytes 1048576
  77.7 6.1 %slice-start.3 = ((s8[4718592]{0:T(1024)(128)(4,1)}), s8[4194304]{0:T(1024)(128)(4,1)S(1)}, s32[]{:S(2)}) async-start(s8[4718592]{0:T(1024)(128)(4,1)} %bitcast.101), calls=%async_computation.5 | async-start | bytes 8388608
  91.6 19.7 %copy-start.11 = (bf16[128,192]{0,1:T(8,128)(2,1)S(1)}, bf16[128,192]{0,1:T(8,128)(2,1)}, u32[]{:S(2)}) copy-start(bf16[128,192]{0,1:T(8,128)(2,1)} %param.9) | copy-start | bytes 147460
  111.3 5.0 %copy-start.4 = (bf16[2,4,192,1024]{3,2,1,0:T(8,128)(2,1)S(1)}, bf16[2,4,192,1024]{3,2,1,0:T(8,128)(2,1)}, u32[]{:S(2)}) copy-start(bf16[2,4,192,1024]{3,2,1,0:T(8,128)(2,1)} %fusion.32) | copy-start | bytes 9437188
  111.3 5.0 %copy-start.12 = (bf16[128,192]{0,1:T(8,128)(2,1)S(1)}, bf16[128,192]{0,1:T(8,128)(2,1)}, u32[]{:S(2)}) copy-start(bf16[128,192]{0,1:T(8,128)(2,1)} %param.8) | copy-start | bytes 147460
  116.0 119.7 %all-gather.3.cloned.1.call-start = ((), (), s32[]{:S(2)}) async-start(), calls=%async_computation | async-start | bytes 10485760 | tf_op jit(solution)/shard_map/all_gather | solution.py:108
  181.8 53.9 %copy-start.1 = (bf16[2,4,1024,128]{3,2,1,0:T(8,128)(2,1)S(1)}, bf16[2,4,1024,128]{3,2,1,0:T(8,128)(2,1)}, u32[]{:S(2)}) copy-start(bf16[2,4,1024,128]{3,2,1,0:T(8,128)(2,1)} %convolution_convert_fusion) | copy-start | bytes 6291460
  311.5 22.6 %copy-start.7 = (bf16[2,4,128,1024]{2,3,1,0:T(8,128)(2,1)S(1)}, bf16[2,4,128,1024]{2,3,1,0:T(8,128)(2,1)}, u32[]{:S(2)}) copy-start(bf16[2,4,128,1024]{2,3,1,0:T(8,128)(2,1)} %slice.155) | copy-start | bytes 6291460
  349.8 3.2 copy-start.6
  368.8 24.9 %copy-start.8 = (f32[2,4,128,1024]{3,2,1,0:T(8,128)S(1)}, f32[2,4,128,1024]{3,2,1,0:T(8,128)}, u32[]{:S(2)}) copy-start(f32[2,4,128,1024]{3,2,1,0:T(8,128)} %fusion.10) | copy-start | bytes 12582916
  368.8 24.9 %copy-start.9 = (f32[2,4,128,1024]{3,2,1,0:T(8,128)S(1)}, f32[2,4,128,1024]{3,2,1,0:T(8,128)}, u32[]{:S(2)}) copy-start(f32[2,4,128,1024]{3,2,1,0:T(8,128)} %fusion.8) | copy-start | bytes 12582916
  393.7 16.8 %copy-start.5 = (bf16[2,4,192,1024]{3,2,1,0:T(8,128)(2,1)S(1)}, bf16[2,4,192,1024]{3,2,1,0:T(8,128)(2,1)}, u32[]{:S(2)}) copy-start(bf16[2,4,192,1024]{3,2,1,0:T(8,128)(2,1)} %fusion.32) | copy-start | bytes 9437188
  393.8 16.8 %copy-start.13 = (f32[128]{0:T(128)S(1)}, f32[128]{0:T(128)}, u32[]{:S(2)}) copy-start(f32[128]{0:T(128)} %param.10) | copy-start | bytes 1540
Sparse Core Ops, SparseCore 0:
  116.2 59.6 all-gather.4
  177.4 58.2 all-gather.2
where the time goes:
time: 424 us; the launch traced here: 420 us
  matrix products  191 us (45%)
  waiting for transfers between devices  127 us (30%)
  other arithmetic  47.6 us (11%)
  local copies, waits for them, and re-layouts  32.4 us (8%)
  between operations  13.8 us (3%)
  starting transfers between devices  8.04 us (2%)
    dot_general x4, matrix products, attend(): jnp.einsum('vrij,vraj->vrai', weights.astype(jnp.bfloat16), value_block,...  64.9 us
    dot_general x4, matrix products, attend(): jnp.einsum('vrai,vraj->vrij', queries, key_block, preferred_element_type=...  59.1 us
    dot_general x9, matrix products, body(): jnp.einsum('oc,vrcw->vrow', conv_weight[3 * row_step + col_step], window,...  57 us
    all_gather x1, waiting for transfers between devices, body(): lax.all_gather(valued, 'lon', axis=3, tiled=True)  56.7 us
    reduce_sum x2, other arithmetic, attend(): running_sum = running_sum * factor + jnp.sum(weights, axis=-1)  47.4 us
    all_gather x1, waiting for transfers between devices, body(): lax.all_gather(matched, 'lon', axis=3, tiled=True)  43.4 us
    ppermute x2, waiting for transfers between devices, with_halo(): lax.ppermute(tail, axis, [(i, (i + 1) % count) for i in range(ends)])  27.2 us
    slice x5, local copies, waits for them, and re-layouts, attend(): value_block = value_rows[..., offset:offset + block_len]  19.7 us
  transfers between devices with their start and end apart: 6, of which 3 were waited for; matrix products, arithmetic and copies ran while one was open for 11% of the time, Pallas kernels for 0%

commit v1 on v0

v1 whole, which is shorter than its diff:
```python
import functools
import math

import jax
import jax.numpy as jnp
from jax import lax
from jax.experimental import pallas as pl
from jax.experimental.pallas import tpu as pltpu
from jax.sharding import PartitionSpec as P

F32 = jnp.float32
BF16 = jnp.bfloat16
VMEM_LIMIT = 56 * 1024 * 1024


def conv_kernel(row, side_ref, xu, xm, xd, eu, em, ed, w_ref, out_ref):
    chan = w_ref.shape[1]
    cols = xm.shape[3]
    y = None
    for step, (x, e) in enumerate(((xu, eu), (xm, em), (xd, ed))):
        w = w_ref[3 * step : 3 * step + 3].reshape(3 * chan, chan)
        xe = jnp.concatenate([x[0, 0], e[0, 0]], axis=1)
        term = jnp.dot(w, xe, preferred_element_type=F32)
        y = term if y is None else y + term
    wide = y.shape[1]
    left = pltpu.roll(y[:chan], 1, axis=1)[:, :cols]
    right = pltpu.roll(y[2 * chan :], wide - 1, axis=1)[:, :cols]
    conv = y[chan : 2 * chan, :cols] + side_ref[row] * (left + right)
    out_ref[0, 0] = (xm[0, 0].astype(F32) + jax.nn.gelu(conv, approximate=True)).astype(BF16)


def conv_row(row, side, parts, edges, conv_weight):
    (_, mid_row) = parts[1]
    chan, cols = parts[1][0].shape[2], parts[1][0].shape[3]

    def spec(index, width):
        return pl.BlockSpec((1, 1, chan, width), lambda v: (v, index, 0, 0))

    return pl.pallas_call(
        functools.partial(conv_kernel, row),
        grid=(2,),
        in_specs=[pl.BlockSpec(memory_space=pltpu.SMEM)]
        + [spec(i, cols) for _, i in parts]
        + [spec(i, 128) for _, i in edges]
        + [pl.BlockSpec(conv_weight.shape, lambda v: (0, 0, 0))],
        out_specs=spec(0, cols),
        out_shape=jax.ShapeDtypeStruct((2, 1, chan, cols), BF16),
        compiler_params=pltpu.CompilerParams(vmem_limit_bytes=VMEM_LIMIT),
        cost_estimate=pl.CostEstimate(
            flops=2 * 2 * 9 * chan * chan * cols,
            bytes_accessed=2 * 2 * 4 * chan * cols,
            transcendentals=2 * chan * cols,
        ),
        name="conv_row",
    )(side, *[x for x, _ in parts], *[e for e, _ in edges], conv_weight)


def attend_kernel(count, tj, tk, *refs):
    own = refs[0]
    blocks = refs[1 : 1 + count]
    wkv, gain, ow = refs[1 + count : 4 + count]
    out_ref, kbuf, vbuf, qbuf, acc = refs[5 + count :]
    chan = wkv.shape[0] // 2
    cols = own.shape[3]
    keys = kbuf.shape[1]
    scale = 1.0 / math.sqrt(chan)
    log2e = 1.4426950408889634
    mult = scale * log2e

    kmax = jnp.zeros((1, cols), F32)
    for b, blk in enumerate(blocks):
        kv = jnp.dot(wkv[...], blk[0, 0], preferred_element_type=F32)
        k16 = kv[:chan].astype(BF16)
        kbuf[:, b * cols : (b + 1) * cols] = k16
        kf = k16.astype(F32)
        kmax = jnp.maximum(kmax, jnp.sum(kf * kf, axis=0, keepdims=True))
        vbuf[b * cols : (b + 1) * cols, :chan] = kv[chan:].T.astype(BF16)
    vbuf[:, chan:] = jnp.ones((keys, chan), BF16)
    q = jnp.dot(wkv[:chan], own[0, 0], preferred_element_type=F32)
    qr = q.astype(BF16).astype(F32)
    qmax = jnp.max(jnp.sum(qr * qr, axis=0, keepdims=True))
    qbuf[...] = q.T.astype(BF16)
    bound = jnp.sqrt(qmax) * jnp.sqrt(jnp.max(kmax)) * scale
    small = bound < 60.0

    def finish(j):
        total = acc[...]
        att = total[:, :chan] / total[:, chan:]
        ms = jnp.mean(att * att, axis=1, keepdims=True)
        normed = (att * lax.rsqrt(ms + 1e-06) * gain[...]).astype(BF16)
        delta = lax.dot_general(
            ow[...], normed, (((1,), (1,)), ((), ())), preferred_element_type=F32
        )
        out_ref[0, 0, :, pl.ds(j, tj)] = (
            own[0, 0, :, pl.ds(j, tj)].astype(F32) + delta
        ).astype(BF16)

    @pl.when(small)
    def _():
        @pl.loop(0, cols // tj)
        def _(step):
            j = pl.multiple_of(step * tj, tj)
            qb = qbuf[pl.ds(j, tj), :]
            total = None
            for kc in range(0, keys, tk):
                s = jnp.dot(qb, kbuf[:, kc : kc + tk], preferred_element_type=F32)
                p = jnp.exp2(s * mult).astype(BF16)
                term = jnp.dot(p, vbuf[kc : kc + tk, :], preferred_element_type=F32)
                total = term if total is None else total + term
            acc[...] = total
            finish(j)

    @pl.when(jnp.logical_not(small))
    def _():
        @pl.loop(0, cols // tj)
        def _(step):
            j = pl.multiple_of(step * tj, tj)
            qb = qbuf[pl.ds(j, tj), :]

            def scores(i):
                kc = pl.multiple_of(i * tk, tk)
                return jnp.dot(qb, kbuf[:, pl.ds(kc, tk)], preferred_element_type=F32) * scale

            peak = lax.fori_loop(
                0,
                keys // tk,
                lambda i, m: jnp.maximum(m, jnp.max(scores(i), axis=1, keepdims=True)),
                jnp.full((tj, 1), -jnp.inf, F32),
            )
            acc[...] = jnp.zeros_like(acc)

            @pl.loop(0, keys // tk)
            def _(i):
                p = jnp.exp(scores(i) - peak).astype(BF16)
                kc = pl.multiple_of(i * tk, tk)
                acc[...] += jnp.dot(p, vbuf[pl.ds(kc, tk), :], preferred_element_type=F32)

            finish(j)


def attend_row(row, own, blocks, wkv, gain, ow, out_buf, out_shape):
    chan, cols = own.shape[2], own.shape[3]
    att = gain.shape[1]
    count = len(blocks)
    keys = count * cols
    tj, tk = min(256, cols), 512

    def whole(a):
        return pl.BlockSpec(a.shape, lambda v: (0,) * a.ndim)

    return pl.pallas_call(
        functools.partial(attend_kernel, count, tj, tk),
        grid=(2,),
        in_specs=[pl.BlockSpec((1, 1, chan, cols), lambda v: (v, 0, 0, 0))]
        + [pl.BlockSpec((1, 1, chan, cols), lambda v: (1 - v, 0, 0, 0))] * count
        + [whole(wkv), whole(gain), whole(ow), pl.BlockSpec(memory_space=pl.ANY)],
        out_specs=pl.BlockSpec((1, 1, chan, cols), lambda v: (v, row, 0, 0)),
        out_shape=jax.ShapeDtypeStruct(out_shape, BF16),
        scratch_shapes=[
            pltpu.VMEM((att, keys), BF16),
            pltpu.VMEM((keys, 2 * att), BF16),
            pltpu.VMEM((cols, att), BF16),
            pltpu.VMEM((tj, 2 * att), F32),
        ],
        input_output_aliases={4 + count: 0},
        compiler_params=pltpu.CompilerParams(vmem_limit_bytes=VMEM_LIMIT),
        cost_estimate=pl.CostEstimate(
            flops=2 * 2 * 2 * 2 * cols * keys * att,
            bytes_accessed=2 * 2 * (count + 2) * chan * cols,
            transcendentals=2 * cols * keys,
        ),
        name="attend_row",
    )(own, *blocks, wkv, gain, ow, out_buf)


def body(views, conv_weight, match_weight, value_weight, post_gain, out_weight):
    _, rows, chan, cols = views.shape
    lat, lon = lax.axis_size("lat"), lax.axis_size("lon")
    forward = [(i, (i + 1) % lon) for i in range(lon)]
    backward = [((i + 1) % lon, i) for i in range(lon)]
    down = [(i, i + 1) for i in range(lat - 1)]
    up = [(i + 1, i) for i in range(lat - 1)]
    swap = [(i, i ^ 1) for i in range(lon)]

    from_left = lax.ppermute(views[..., cols - 1], "lon", forward)
    from_right = lax.ppermute(views[..., 0], "lon", backward)
    edges = jnp.concatenate(
        [
            from_right[..., None],
            jnp.zeros((2, rows, chan, 126), BF16),
            from_left[..., None],
        ],
        axis=3,
    )
    top = lax.ppermute(views[:, rows - 1 :], "lat", down)
    bottom = lax.ppermute(views[:, :1], "lat", up)
    edge_top = lax.ppermute(edges[:, rows - 1 :], "lat", down)
    edge_bottom = lax.ppermute(edges[:, :1], "lat", up)

    row_total = rows * lat
    row_index = (lax.axis_index("lat") * rows + jnp.arange(rows, dtype=jnp.int32)).astype(F32)
    latitude = (row_index + 0.5 - 0.5 * row_total) * (2.8 / row_total)
    side = 1.0 / (jnp.cos(latitude) + 0.25)
    wkv = jnp.concatenate([match_weight, value_weight], axis=0)
    gain = post_gain[None, :]

    def source(r, own, first, last):
        if r < 0:
            return (first, 0)
        if r >= rows:
            return (last, 0)
        return (own, r)

    order = list(range(1, rows - 1)) + [0, rows - 1]
    gathered = []
    for r in order:
        parts = [source(r + a, views, top, bottom) for a in (-1, 0, 1)]
        sides = [source(r + a, edges, edge_top, edge_bottom) for a in (-1, 0, 1)]
        own = conv_row(r, side, parts, sides, conv_weight)
        same_core = [own]
        for s in range(1, lon // 2):
            same_core.append(
                lax.ppermute(own, "lon", [(i, (i + 2 * s) % lon) for i in range(lon)])
            )
        other_core = [lax.ppermute(b, "lon", swap) for b in same_core]
        gathered.append((r, own, same_core + other_core))
    out = jnp.zeros(views.shape, BF16)
    for r, own, blocks in gathered:
        out = attend_row(r, own, blocks, wkv, gain, out_weight, out, views.shape)
    return out


def solution(mesh):
    placed = (P(None, "lat", None, "lon"), P(), P(), P(), P(), P())
    return jax.shard_map(
        body, mesh=mesh, in_specs=placed, out_specs=P(None, "lat", None, "lon"), check_vma=False
    )
```

time: 424 us -> 283 us (0.67)
  Pallas kernels: 0 us -> 223 us
  matrix products: 191 us -> 0 us
  waiting for transfers between devices: 127 us -> 30 us
  other arithmetic: 47.6 us -> 2.25 us
  local copies, waits for them, and re-layouts: 32.4 us -> 8.61 us
  between operations: 13.8 us -> 0.23 us
  starting transfers between devices: 8.04 us -> 18.2 us
    pallas_call x0 -> x8, Pallas kernels: none -> 223 us  [the longest x4 199 us: attend_row(): pl.pallas_call(functools.partial(attend_kernel, count, tj, tk), grid=(2,)...]
    dot_general x20 -> x0, matrix products: 191 us -> none  [the longest x4 64.9 us: attend(): jnp.einsum('vrij,vraj->vrai', weights.astype(jnp.bfloat16), value_block,...]
    all_gather x2 -> x0, waiting for transfers between devices: 100 us -> none  [the longest x1 56.7 us: body(): lax.all_gather(valued, 'lon', axis=3, tiled=True)]
    reduce_sum x2 -> x0, other arithmetic: 47.4 us -> none  [attend(): running_sum = running_sum * factor + jnp.sum(weights, axis=-1)]
    slice x9 -> x3, local copies, waits for them, and re-layouts: 26.5 us -> 2.9 us  [the longest x1 1.6 us: body(): from_right = lax.ppermute(views[..., 0], 'lon', backward)]
    ppermute x4 -> x18, starting transfers between devices: 7.78 us -> 18.2 us  [the longest x1 4.68 us: body(): edge_top = lax.ppermute(edges[:, rows - 1:], 'lat', down)]
    ppermute x4 -> x18, waiting for transfers between devices: 27.2 us -> 30 us  [the longest x1 23.9 us: body(): edge_top = lax.ppermute(edges[:, rows - 1:], 'lat', down)]
  transfers between devices with their start and end apart: 6 -> 18, of which waited for: 3 -> 5; matrix products, arithmetic and copies ran while one was open for 11% -> 2% of each run, Pallas kernels for 0% -> 59%
where the time goes in v1:
time: 283 us; the launch traced here: 282 us
  Pallas kernels  223 us (79%)
  waiting for transfers between devices  30 us (11%)
  starting transfers between devices  18.2 us (6%)
  local copies, waits for them, and re-layouts  8.61 us (3%)
    pallas_call x4, Pallas kernels, attend_row(): pl.pallas_call(functools.partial(attend_kernel, count, tj, tk), grid=(2,)...  199 us
    ppermute x1, waiting for transfers between devices, body(): edge_top = lax.ppermute(edges[:, rows - 1:], 'lat', down)  23.9 us
    pallas_call x4, Pallas kernels, conv_row(): pl.pallas_call(functools.partial(conv_kernel, row), grid=(2,), in_specs=[...  23.6 us
  transfers between devices with their start and end apart: 18, of which 5 were waited for; matrix products, arithmetic and copies ran while one was open for 2% of the time, Pallas kernels for 59%

profile of v1, /device:TPU:0, one launch (start us, length us, event | category | flops | bytes accessed | tf_op | source)
XLA Modules:
  0.0 282.2 jit_solution(1333294593688548420)
XLA Ops:
  0.0 1.6 slice_reduce_fusion.1
  1.6 2.4 collective-permute-start.1
  4.0 0.6 add_divide_fusion.side_ref
  4.7 0.7 collective-permute-done.1
  5.7 1.4 collective-permute-done.2
  7.4 1.0 pad_maximum_fusion.eu.em.ed
  8.3 6.0 %conv_row.7.refs_0_.refs_1_ = bf16[2,1,192,1024]{3,2,1,0:T(8,128)(2,1)} custom-call(f32[4]{0:T(128)} %add_divide_fusion.side_ref, bf16[2,4,192,1024]{3,2,1,0:T(8,128)(2,1)} %xd.5, bf16[2,4,192,1024]{3,2,1,0:T(8,128)(2,1)} %xd.5, bf16[2,4,192,1024]{3,2,1,0:T(8,128)(2,1)} %xd.5, bf16[2,4,192,128]{3,2,1,0:T(8,128)(2,1)} %pad_maximum_fusion.eu.em.ed, ...), custom_call_target="tpu_custom_call" | custom-call | flops 1358954496 | bytes 3145728 | tf_op jit(solution)/shard_map/conv_row/pallas_call | solution.py:39
  14.3 0.7 collective-permute-start.15
  15.0 1.3 fusion
  16.3 3.5 %collective-permute-start.7 = (bf16[2,1,192,1024]{3,2,1,0:T(8,128)(2,1)}, bf16[2,1,192,1024]{3,2,1,0:T(8,128)(2,1)S(1)}, u32[]{:S(2)}, u32[]{:S(2)}) collective-permute-start(bf16[2,1,192,1024]{3,2,1,0:T(8,128)(2,1)} %get-tuple-element.7), channel_id=1, source_target_pairs={{0,4},{4,8},{8,12},{12,16},{16,20},{20,24},{24,28},{1,5},{5,9},{9,... | collective-permute-start | bytes 2359304 | tf_op jit(solution)/shard_map/ppermute | solution.py:195
  19.8 1.3 collective-permute-start
  21.2 4.7 %collective-permute-start.8 = (bf16[2,1,192,128]{3,2,1,0:T(8,128)(2,1)S(1)}, bf16[2,1,192,128]{3,2,1,0:T(8,128)(2,1)S(1)}, u32[]{:S(2)}, u32[]{:S(2)}) collective-permute-start(bf16[2,1,192,128]{3,2,1,0:T(8,128)(2,1)S(1)} %get-tuple-element.9), channel_id=1, source_target_pairs={{0,4},{4,8},{8,12},{12,16},{16,20},{20,24},{24,28},{1,5},{5,9},{9,... | collective-permute-start | bytes 294920 | tf_op jit(solution)/shard_map/ppermute | solution.py:197
  25.9 5.9 %conv_row.6.refs_0_.refs_1_ = bf16[2,1,192,1024]{3,2,1,0:T(8,128)(2,1)} custom-call(f32[4]{0:T(128)} %add_divide_fusion.side_ref, bf16[2,4,192,1024]{3,2,1,0:T(8,128)(2,1)} %xd.5, bf16[2,4,192,1024]{3,2,1,0:T(8,128)(2,1)} %xd.5, bf16[2,4,192,1024]{3,2,1,0:T(8,128)(2,1)} %xd.5, bf16[2,4,192,128]{3,2,1,0:T(8,128)(2,1)} %pad_maximum_fusion.eu.em.ed, ...), custom_call_target="tpu_custom_call" | custom-call | flops 1358954496 | bytes 3145728 | tf_op jit(solution)/shard_map/conv_row/pallas_call | solution.py:39
  31.8 23.9 %collective-permute-done.8.eu = bf16[2,1,192,128]{3,2,1,0:T(8,128)(2,1)S(1)} collective-permute-done((bf16[2,1,192,128]{3,2,1,0:T(8,128)(2,1)S(1)}, bf16[2,1,192,128]{3,2,1,0:T(8,128)(2,1)S(1)}, u32[]{:S(2)}, u32[]{:S(2)}) %collective-permute-start.8) | collective-permute-done | bytes 98336 | tf_op jit(solution)/shard_map/ppermute | solution.py:197
  55.6 0.6 collective-permute-start.12
  56.4 0.7 pad_maximum_fusion.1.refs_5_
  57.1 1.6 collective-permute-start.3
  58.7 5.9 %conv_row.5.refs_0_.refs_1_ = bf16[2,1,192,1024]{3,2,1,0:T(8,128)(2,1)} custom-call(f32[4]{0:T(128)} %add_divide_fusion.side_ref, bf16[2,1,192,1024]{3,2,1,0:T(8,128)(2,1)} %copy-done.6, bf16[2,4,192,1024]{3,2,1,0:T(8,128)(2,1)} %xd.5, bf16[2,4,192,1024]{3,2,1,0:T(8,128)(2,1)} %xd.5, bf16[2,1,192,128]{3,2,1,0:T(8,128)(2,1)} %copy-done.7, ...), custom_call_target="tpu_custom_call" | custom-call | flops 1358954496 | bytes 3145728 | tf_op jit(solution)/shard_map/conv_row/pallas_call | solution.py:39
  64.6 0.5 collective-permute-done.3.ed
  65.2 1.5 collective-permute-start.9
  66.7 5.9 %conv_row.4.refs_0_.refs_1_ = bf16[2,1,192,1024]{3,2,1,0:T(8,128)(2,1)} custom-call(f32[4]{0:T(128)} %add_divide_fusion.side_ref, bf16[2,4,192,1024]{3,2,1,0:T(8,128)(2,1)} %xd.5, bf16[2,4,192,1024]{3,2,1,0:T(8,128)(2,1)} %xd.5, bf16[2,1,192,1024]{3,2,1,0:T(8,128)(2,1)} %copy-done.5, bf16[2,4,192,128]{3,2,1,0:T(8,128)(2,1)} %pad_maximum_fusion.eu.em.ed, ...), custom_call_target="tpu_custom_call" | custom-call | flops 1358954496 | bytes 3145728 | tf_op jit(solution)/shard_map/conv_row/pallas_call | solution.py:39
  72.8 3.5 %collective-permute-done.12.refs_2_ = bf16[2,1,192,1024]{3,2,1,0:T(8,128)(2,1)S(1)} collective-permute-done((bf16[2,1,192,1024]{3,2,1,0:T(8,128)(2,1)}, bf16[2,1,192,1024]{3,2,1,0:T(8,128)(2,1)S(1)}, u32[]{:S(2)}, u32[]{:S(2)}) %collective-permute-start.12) | collective-permute-done | bytes 786464 | tf_op jit(solution)/shard_map/ppermute | solution.py:223
  76.3 0.6 collective-permute-start.4
  76.9 2.1 broadcast_in_dim.19.refs_8_
  79.0 49.9 %attend_row.4.refs_8_ = bf16[2,4,192,1024]{3,2,1,0:T(8,128)(2,1)} custom-call(bf16[2,1,192,1024]{3,2,1,0:T(8,128)(2,1)} %conv_row.7.refs_0_.refs_1_, bf16[2,1,192,1024]{3,2,1,0:T(8,128)(2,1)} %conv_row.7.refs_0_.refs_1_, bf16[2,1,192,1024]{3,2,1,0:T(8,128)(2,1)} %collective-permute-done.15.refs_2_, ...), custom_call_target="tpu_custom_call", output_to_operand_aliasing={{}: (8, {})} | custom-call | flops 8589934592 | bytes 4718592 | tf_op jit(solution)/shard_map/attend_row/pallas_call | solution.py:151
  128.9 0.5 collective-permute-start.5
  130.0 0.9 copy-done.17
  130.9 49.8 %attend_row.5.refs_8_ = bf16[2,4,192,1024]{3,2,1,0:T(8,128)(2,1)} custom-call(bf16[2,1,192,1024]{3,2,1,0:T(8,128)(2,1)} %conv_row.6.refs_0_.refs_1_, bf16[2,1,192,1024]{3,2,1,0:T(8,128)(2,1)} %conv_row.6.refs_0_.refs_1_, bf16[2,1,192,1024]{3,2,1,0:T(8,128)(2,1)} %copy-done.11, bf16[2,1,192,1024]{3,2,1,0:T(8,128)(2,1)} %copy-done.13, ...), custom_call_target="tpu_custom_call", output_to_operand_aliasing={{}: (8, {})} | custom-call | flops 8589934592 | bytes 4718592 | tf_op jit(solution)/shard_map/attend_row/pallas_call | solution.py:151
  180.7 0.9 copy-done.15
  181.6 49.8 %attend_row.6.refs_8_ = bf16[2,4,192,1024]{3,2,1,0:T(8,128)(2,1)} custom-call(bf16[2,1,192,1024]{3,2,1,0:T(8,128)(2,1)} %conv_row.5.refs_0_.refs_1_, bf16[2,1,192,1024]{3,2,1,0:T(8,128)(2,1)} %conv_row.5.refs_0_.refs_1_, bf16[2,1,192,1024]{3,2,1,0:T(8,128)(2,1)} %copy-done.12, bf16[2,1,192,1024]{3,2,1,0:T(8,128)(2,1)} %copy-done.15, ...), custom_call_target="tpu_custom_call", output_to_operand_aliasing={{}: (8, {})} | custom-call | flops 8589934592 | bytes 4718592 | tf_op jit(solution)/shard_map/attend_row/pallas_call | solution.py:151
  231.4 0.9 copy-done.16
  232.4 49.8 %attend_row.7 = bf16[2,4,192,1024]{3,2,1,0:T(8,128)(2,1)} custom-call(bf16[2,1,192,1024]{3,2,1,0:T(8,128)(2,1)} %conv_row.4.refs_0_.refs_1_, bf16[2,1,192,1024]{3,2,1,0:T(8,128)(2,1)} %conv_row.4.refs_0_.refs_1_, bf16[2,1,192,1024]{3,2,1,0:T(8,128)(2,1)} %copy-done.14, bf16[2,1,192,1024]{3,2,1,0:T(8,128)(2,1)} %copy-done.16, ...), custom_call_target="tpu_custom_call", output_to_operand_aliasing={{}: (8, {})} | custom-call | flops 8589934592 | bytes 4718592 | tf_op jit(solution)/shard_map/attend_row/pallas_call | solution.py:151
  (61 shorter events, 1.9 us)
Async XLA Ops:
  1.6 3.8 %collective-permute-start.1 = (bf16[2,4,192]{2,1,0:T(4,128)(2,1)S(1)}, bf16[2,4,192]{2,1,0:T(4,128)(2,1)S(1)}, u32[]{:S(2)}, u32[]{:S(2)}) collective-permute-start(bf16[2,4,192]{2,1,0:T(4,128)(2,1)S(1)} %get-tuple-element.5), channel_id=1, source_target_pairs={{1,0},{2,1},{3,2},{0,3},{5,4},{6,5},{7,6},{4,7},{9,8},{10,9},{11,1... | collective-permute-start | bytes 9224 | tf_op jit(solution)/shard_map/ppermute | solution.py:186
  4.0 3.0 %collective-permute-start.2 = (bf16[2,4,192]{2,1,0:T(4,128)(2,1)S(1)}, bf16[2,4,192]{2,1,0:T(4,128)(2,1)S(1)}, u32[]{:S(2)}, u32[]{:S(2)}) collective-permute-start(bf16[2,4,192]{2,1,0:T(4,128)(2,1)S(1)} %get-tuple-element.6), channel_id=1, source_target_pairs={{0,1},{1,2},{2,3},{3,0},{4,5},{5,6},{6,7},{7,4},{8,9},{9,10},{10,1... | collective-permute-start | bytes 9224 | tf_op jit(solution)/shard_map/ppermute | solution.py:185
  8.3 6.7 %copy-start = (bf16[2,4,192,1024]{3,2,1,0:T(8,128)(2,1)S(1)}, bf16[2,4,192,1024]{3,2,1,0:T(8,128)(2,1)}, u32[]{:S(2)}) copy-start(bf16[2,4,192,1024]{3,2,1,0:T(8,128)(2,1)} %xd.5) | copy-start | bytes 9437188
  14.3 6.8 %copy-start.1 = (bf16[2,4,192,128]{3,2,1,0:T(8,128)(2,1)S(1)}, bf16[2,4,192,128]{3,2,1,0:T(8,128)(2,1)}, u32[]{:S(2)}) copy-start(bf16[2,4,192,128]{3,2,1,0:T(8,128)(2,1)} %pad_maximum_fusion.eu.em.ed) | copy-start | bytes 1179652
  14.3 41.9 %collective-permute-start.15 = (bf16[2,1,192,1024]{3,2,1,0:T(8,128)(2,1)}, bf16[2,1,192,1024]{3,2,1,0:T(8,128)(2,1)}, u32[]{:S(2)}, u32[]{:S(2)}) collective-permute-start(bf16[2,1,192,1024]{3,2,1,0:T(8,128)(2,1)} %conv_row.7.refs_0_.refs_1_), channel_id=1, source_target_pairs={{0,2},{1,3},{2,0},{3,1},{4,6},{5,7},{6,4},{7,5},{8,10},{9,11},{10,... | collective-permute-start | bytes 2359304 | tf_op jit(solution)/shard_map/ppermute | solution.py:223
  16.3 40.8 %collective-permute-start.7 = (bf16[2,1,192,1024]{3,2,1,0:T(8,128)(2,1)}, bf16[2,1,192,1024]{3,2,1,0:T(8,128)(2,1)S(1)}, u32[]{:S(2)}, u32[]{:S(2)}) collective-permute-start(bf16[2,1,192,1024]{3,2,1,0:T(8,128)(2,1)} %get-tuple-element.7), channel_id=1, source_target_pairs={{0,4},{4,8},{8,12},{12,16},{16,20},{20,24},{24,28},{1,5},{5,9},{9,... | collective-permute-start | bytes 2359304 | tf_op jit(solution)/shard_map/ppermute | solution.py:195
  19.8 45.4 %collective-permute-start = (bf16[2,1,192,1024]{3,2,1,0:T(8,128)(2,1)}, bf16[2,1,192,1024]{3,2,1,0:T(8,128)(2,1)S(1)}, u32[]{:S(2)}, u32[]{:S(2)}) collective-permute-start(bf16[2,1,192,1024]{3,2,1,0:T(8,128)(2,1)} %get-tuple-element.8), channel_id=1, source_target_pairs={{4,0},{8,4},{12,8},{16,12},{20,16},{24,20},{28,24},{5,1},{9,5},{13... | collective-permute-start | bytes 2359304 | tf_op jit(solution)/shard_map/ppermute | solution.py:196
  21.1 51.5 %collective-permute-start.16 = (bf16[2,1,192,1024]{3,2,1,0:T(8,128)(2,1)}, bf16[2,1,192,1024]{3,2,1,0:T(8,128)(2,1)}, u32[]{:S(2)}, u32[]{:S(2)}) collective-permute-start(bf16[2,1,192,1024]{3,2,1,0:T(8,128)(2,1)} %conv_row.7.refs_0_.refs_1_), channel_id=1, source_target_pairs={{0,1},{1,0},{2,3},{3,2},{4,5},{5,4},{6,7},{7,6},{8,9},{9,8},{10,11... | collective-permute-start | bytes 2359304 | tf_op jit(solution)/shard_map/ppermute | solution.py:225
  21.2 35.0 %copy-start.9 = (bf16[128,192]{0,1:T(8,128)(2,1)S(1)}, bf16[128,192]{0,1:T(8,128)(2,1)}, u32[]{:S(2)}) copy-start(bf16[128,192]{0,1:T(8,128)(2,1)} %param.8) | copy-start | bytes 147460
  21.2 35.1 %copy-start.10 = (bf16[128,192]{0,1:T(8,128)(2,1)S(1)}, bf16[128,192]{0,1:T(8,128)(2,1)}, u32[]{:S(2)}) copy-start(bf16[128,192]{0,1:T(8,128)(2,1)} %param.9) | copy-start | bytes 147460
  21.2 34.4 %collective-permute-start.8 = (bf16[2,1,192,128]{3,2,1,0:T(8,128)(2,1)S(1)}, bf16[2,1,192,128]{3,2,1,0:T(8,128)(2,1)S(1)}, u32[]{:S(2)}, u32[]{:S(2)}) collective-permute-start(bf16[2,1,192,128]{3,2,1,0:T(8,128)(2,1)S(1)} %get-tuple-element.9), channel_id=1, source_target_pairs={{0,4},{4,8},{8,12},{12,16},{16,20},{20,24},{24,28},{1,5},{5,9},{9,... | collective-permute-start | bytes 294920 | tf_op jit(solution)/shard_map/ppermute | solution.py:197
  55.6 3.1 %copy-start.7 = (bf16[2,1,192,128]{3,2,1,0:T(8,128)(2,1)}, bf16[2,1,192,128]{3,2,1,0:T(8,128)(2,1)S(1)}, u32[]{:S(2)}) copy-start(bf16[2,1,192,128]{3,2,1,0:T(8,128)(2,1)S(1)} %collective-permute-done.8.eu) | copy-start | bytes 294916
  55.6 20.7 %collective-permute-start.12 = (bf16[2,1,192,1024]{3,2,1,0:T(8,128)(2,1)}, bf16[2,1,192,1024]{3,2,1,0:T(8,128)(2,1)S(1)}, u32[]{:S(2)}, u32[]{:S(2)}) collective-permute-start(bf16[2,1,192,1024]{3,2,1,0:T(8,128)(2,1)} %conv_row.6.refs_0_.refs_1_), channel_id=1, source_target_pairs={{0,2},{1,3},{2,0},{3,1},{4,6},{5,7},{6,4},{7,5},{8,10},{9,11},{10,... | collective-permute-start | bytes 2359304 | tf_op jit(solution)/shard_map/ppermute | solution.py:223
  56.2 20.7 %collective-permute-start.17 = (bf16[2,1,192,1024]{3,2,1,0:T(8,128)(2,1)}, bf16[2,1,192,1024]{3,2,1,0:T(8,128)(2,1)}, u32[]{:S(2)}, u32[]{:S(2)}) collective-permute-start(bf16[2,1,192,1024]{3,2,1,0:T(8,128)(2,1)} %collective-permute-done.15.refs_2_), channel_id=1, source_target_pairs={{0,1},{1,0},{2,3},{3,2},{4,5},{5,4},{6,7},{7,6},{8,9},{9,8},{10,11... | collective-permute-start | bytes 2359304 | tf_op jit(solution)/shard_map/ppermute | solution.py:225
  57.1 1.6 copy-start.6
  57.1 8.0 %copy-start.2 = (bf16[2,1,192,1024]{3,2,1,0:T(8,128)(2,1)S(1)}, bf16[2,1,192,1024]{3,2,1,0:T(8,128)(2,1)}, u32[]{:S(2)}) copy-start(bf16[2,1,192,1024]{3,2,1,0:T(8,128)(2,1)} %conv_row.6.refs_0_.refs_1_) | copy-start | bytes 2359300
  57.1 8.0 %collective-permute-start.3 = (bf16[2,1,192,128]{3,2,1,0:T(8,128)(2,1)S(1)}, bf16[2,1,192,128]{3,2,1,0:T(8,128)(2,1)S(1)}, u32[]{:S(2)}, u32[]{:S(2)}) collective-permute-start(bf16[2,1,192,128]{3,2,1,0:T(8,128)(2,1)S(1)} %get-tuple-element.10), channel_id=1, source_target_pairs={{4,0},{8,4},{12,8},{16,12},{20,16},{24,20},{28,24},{5,1},{9,5},{13... | collective-permute-start | bytes 294920 | tf_op jit(solution)/shard_map/ppermute | solution.py:198
  64.6 7.9 %copy-start.3 = (bf16[2,1,192,1024]{3,2,1,0:T(8,128)(2,1)S(1)}, bf16[2,1,192,1024]{3,2,1,0:T(8,128)(2,1)}, u32[]{:S(2)}) copy-start(bf16[2,1,192,1024]{3,2,1,0:T(8,128)(2,1)} %conv_row.5.refs_0_.refs_1_) | copy-start | bytes 2359300
  65.1 1.6 copy-start.8
  65.1 63.8 %collective-permute-start.13 = (bf16[2,1,192,1024]{3,2,1,0:T(8,128)(2,1)S(1)}, bf16[2,1,192,1024]{3,2,1,0:T(8,128)(2,1)S(1)}, u32[]{:S(2)}, u32[]{:S(2)}) collective-permute-start(bf16[2,1,192,1024]{3,2,1,0:T(8,128)(2,1)S(1)} %copy-done.2), channel_id=1, source_target_pairs={{0,1},{1,0},{2,3},{3,2},{4,5},{5,4},{6,7},{7,6},{8,9},{9,8},{10,11... | collective-permute-start | bytes 2359304 | tf_op jit(solution)/shard_map/ppermute | solution.py:225
  65.2 1.5 copy-start.5
  65.2 64.2 %collective-permute-start.9 = (bf16[2,1,192,1024]{3,2,1,0:T(8,128)(2,1)}, bf16[2,1,192,1024]{3,2,1,0:T(8,128)(2,1)S(1)}, u32[]{:S(2)}, u32[]{:S(2)}) collective-permute-start(bf16[2,1,192,1024]{3,2,1,0:T(8,128)(2,1)} %conv_row.5.refs_0_.refs_1_), channel_id=1, source_target_pairs={{0,2},{1,3},{2,0},{3,1},{4,6},{5,7},{6,4},{7,5},{8,10},{9,11},{10,... | collective-permute-start | bytes 2359304 | tf_op jit(solution)/shard_map/ppermute | solution.py:223
  72.6 108.2 %collective-permute-start.10 = (bf16[2,1,192,1024]{3,2,1,0:T(8,128)(2,1)S(1)}, bf16[2,1,192,1024]{3,2,1,0:T(8,128)(2,1)S(1)}, u32[]{:S(2)}, u32[]{:S(2)}) collective-permute-start(bf16[2,1,192,1024]{3,2,1,0:T(8,128)(2,1)S(1)} %copy-done.3), channel_id=1, source_target_pairs={{0,1},{1,0},{2,3},{3,2},{4,5},{5,4},{6,7},{7,6},{8,9},{9,8},{10,11... | collective-permute-start | bytes 2359304 | tf_op jit(solution)/shard_map/ppermute | solution.py:225
  76.3 52.6 %copy-start.11 = (bf16[2,1,192,1024]{3,2,1,0:T(8,128)(2,1)}, bf16[2,1,192,1024]{3,2,1,0:T(8,128)(2,1)S(1)}, u32[]{:S(2)}) copy-start(bf16[2,1,192,1024]{3,2,1,0:T(8,128)(2,1)S(1)} %collective-permute-done.12.refs_2_) | copy-start | bytes 2359300
  76.3 53.2 %collective-permute-start.4 = (bf16[2,1,192,1024]{3,2,1,0:T(8,128)(2,1)}, bf16[2,1,192,1024]{3,2,1,0:T(8,128)(2,1)S(1)}, u32[]{:S(2)}, u32[]{:S(2)}) collective-permute-start(bf16[2,1,192,1024]{3,2,1,0:T(8,128)(2,1)} %conv_row.4.refs_0_.refs_1_), channel_id=1, source_target_pairs={{0,2},{1,3},{2,0},{3,1},{4,6},{5,7},{6,4},{7,5},{8,10},{9,11},{10,... | collective-permute-start | bytes 2359304 | tf_op jit(solution)/shard_map/ppermute | solution.py:223
  76.9 53.1 %collective-permute-start.14 = (bf16[2,1,192,1024]{3,2,1,0:T(8,128)(2,1)S(1)}, bf16[2,1,192,1024]{3,2,1,0:T(8,128)(2,1)S(1)}, u32[]{:S(2)}, u32[]{:S(2)}) collective-permute-start(bf16[2,1,192,1024]{3,2,1,0:T(8,128)(2,1)S(1)} %collective-permute-done.12.refs_2_), channel_id=1, source_target_pairs={{0,1},{1,0},{2,3},{3,2},{4,5},{5,4},{6,7},{7,6},{8,9},{9,8},{10,11... | collective-permute-start | bytes 2359304 | tf_op jit(solution)/shard_map/ppermute | solution.py:225
  79.0 49.9 %copy-start.4 = (bf16[2,1,192,1024]{3,2,1,0:T(8,128)(2,1)S(1)}, bf16[2,1,192,1024]{3,2,1,0:T(8,128)(2,1)}, u32[]{:S(2)}) copy-start(bf16[2,1,192,1024]{3,2,1,0:T(8,128)(2,1)} %conv_row.4.refs_0_.refs_1_) | copy-start | bytes 2359300
  128.9 102.5 %collective-permute-start.5 = (bf16[2,1,192,1024]{3,2,1,0:T(8,128)(2,1)S(1)}, bf16[2,1,192,1024]{3,2,1,0:T(8,128)(2,1)S(1)}, u32[]{:S(2)}, u32[]{:S(2)}) collective-permute-start(bf16[2,1,192,1024]{3,2,1,0:T(8,128)(2,1)S(1)} %copy-done.4), channel_id=1, source_target_pairs={{0,1},{1,0},{2,3},{3,2},{4,5},{5,4},{6,7},{7,6},{8,9},{9,8},{10,11... | collective-permute-start | bytes 2359304 | tf_op jit(solution)/shard_map/ppermute | solution.py:225
  129.4 51.3 %copy-start.12 = (bf16[2,1,192,1024]{3,2,1,0:T(8,128)(2,1)}, bf16[2,1,192,1024]{3,2,1,0:T(8,128)(2,1)S(1)}, u32[]{:S(2)}) copy-start(bf16[2,1,192,1024]{3,2,1,0:T(8,128)(2,1)S(1)} %collective-permute-done.9.refs_2_) | copy-start | bytes 2359300
  129.4 51.3 %collective-permute-start.11 = (bf16[2,1,192,1024]{3,2,1,0:T(8,128)(2,1)S(1)}, bf16[2,1,192,1024]{3,2,1,0:T(8,128)(2,1)}, u32[]{:S(2)}, u32[]{:S(2)}) collective-permute-start(bf16[2,1,192,1024]{3,2,1,0:T(8,128)(2,1)S(1)} %collective-permute-done.9.refs_2_), channel_id=1, source_target_pairs={{0,1},{1,0},{2,3},{3,2},{4,5},{5,4},{6,7},{7,6},{8,9},{9,8},{10,11... | collective-permute-start | bytes 2359304 | tf_op jit(solution)/shard_map/ppermute | solution.py:225
  129.5 51.2 %copy-start.14 = (bf16[2,1,192,1024]{3,2,1,0:T(8,128)(2,1)}, bf16[2,1,192,1024]{3,2,1,0:T(8,128)(2,1)S(1)}, u32[]{:S(2)}) copy-start(bf16[2,1,192,1024]{3,2,1,0:T(8,128)(2,1)S(1)} %collective-permute-done.4.refs_2_) | copy-start | bytes 2359300
  129.5 101.9 %collective-permute-start.6 = (bf16[2,1,192,1024]{3,2,1,0:T(8,128)(2,1)S(1)}, bf16[2,1,192,1024]{3,2,1,0:T(8,128)(2,1)}, u32[]{:S(2)}, u32[]{:S(2)}) collective-permute-start(bf16[2,1,192,1024]{3,2,1,0:T(8,128)(2,1)S(1)} %collective-permute-done.4.refs_2_), channel_id=1, source_target_pairs={{0,1},{1,0},{2,3},{3,2},{4,5},{5,4},{6,7},{7,6},{8,9},{9,8},{10,11... | collective-permute-start | bytes 2359304 | tf_op jit(solution)/shard_map/ppermute | solution.py:225
  (4 other events, 3.8 us)

commit v2 on v1

v2 whole, which is shorter than its diff:
```python
import functools
import math

import jax
import jax.numpy as jnp
from jax import lax
from jax.experimental import pallas as pl
from jax.experimental.pallas import tpu as pltpu
from jax.sharding import PartitionSpec as P

F32 = jnp.float32
BF16 = jnp.bfloat16
VMEM_LIMIT = 56 * 1024 * 1024


def conv_kernel(row, side_ref, xu, xm, xd, eu, em, ed, w_ref, *refs):
    out_ref = refs[-1]
    chan = w_ref.shape[1]
    cols = xm.shape[3]
    w = jnp.concatenate(
        [w_ref[3 * a : 3 * a + 3].reshape(3 * chan, chan) for a in range(3)], axis=1
    )
    xe = jnp.concatenate(
        [jnp.concatenate([x[0, 0], e[0, 0]], axis=1) for x, e in ((xu, eu), (xm, em), (xd, ed))],
        axis=0,
    )
    y = jnp.dot(w, xe, preferred_element_type=F32)
    wide = y.shape[1]
    left = pltpu.roll(y[:chan], 1, axis=1)[:, :cols]
    right = pltpu.roll(y[2 * chan :], wide - 1, axis=1)[:, :cols]
    conv = y[chan : 2 * chan, :cols] + side_ref[row] * (left + right)
    out_ref[0, 0] = (xm[0, 0].astype(F32) + jax.nn.gelu(conv, approximate=True)).astype(BF16)


def conv_row(row, side, parts, edges, conv_weight, after):
    chan, cols = parts[1][0].shape[2], parts[1][0].shape[3]

    def spec(index, width):
        return pl.BlockSpec((1, 1, chan, width), lambda v: (v, index, 0, 0))

    return pl.pallas_call(
        functools.partial(conv_kernel, row),
        grid=(2,),
        in_specs=[pl.BlockSpec(memory_space=pltpu.SMEM)]
        + [spec(i, cols) for _, i in parts]
        + [spec(i, 128) for _, i in edges]
        + [pl.BlockSpec(conv_weight.shape, lambda v: (0, 0, 0))]
        + [pl.BlockSpec(memory_space=pl.ANY) for _ in after],
        out_specs=spec(0, cols),
        out_shape=jax.ShapeDtypeStruct((2, 1, chan, cols), BF16),
        compiler_params=pltpu.CompilerParams(vmem_limit_bytes=VMEM_LIMIT),
        cost_estimate=pl.CostEstimate(
            flops=2 * 2 * 9 * chan * chan * cols,
            bytes_accessed=2 * 2 * 4 * chan * cols,
            transcendentals=2 * chan * cols,
        ),
        name="conv_row",
    )(side, *[x for x, _ in parts], *[e for e, _ in edges], conv_weight, *after)


def attend_kernel(count, tj, tk, *refs):
    own = refs[0]
    blocks = refs[1 : 1 + count]
    wkv, gain, ow = refs[1 + count : 4 + count]
    out_ref, token, kbuf, vbuf, qbuf, acc = refs[5 + count :]
    chan = wkv.shape[0] // 2
    cols = own.shape[3]
    keys = kbuf.shape[0]
    scale = 1.0 / math.sqrt(chan)
    mult = scale * 1.4426950408889634

    token[...] = jnp.zeros_like(token)
    kmax = jnp.zeros((1, cols), F32)
    for b, blk in enumerate(blocks):
        kv = jnp.dot(wkv[...], blk[0, 0], preferred_element_type=F32)
        k16 = kv[:chan].astype(BF16)
        kf = k16.astype(F32)
        kmax = jnp.maximum(kmax, jnp.sum(kf * kf, axis=0, keepdims=True))
        kbuf[b * cols : (b + 1) * cols, :] = k16.T
        vbuf[:chan, b * cols : (b + 1) * cols] = kv[chan:].astype(BF16)
    vbuf[chan:, :] = jnp.ones((16, keys), BF16)
    q16 = jnp.dot(wkv[:chan], own[0, 0], preferred_element_type=F32).astype(BF16)
    qr = q16.astype(F32)
    qmax = jnp.max(jnp.sum(qr * qr, axis=0, keepdims=True))
    qbuf[...] = q16
    bound = jnp.sqrt(qmax) * jnp.sqrt(jnp.max(kmax)) * scale
    small = bound < 60.0

    def finish(j, total):
        att = total[:chan] / total[chan : chan + 1]
        ms = jnp.mean(att * att, axis=0, keepdims=True)
        normed = (att * lax.rsqrt(ms + 1e-06) * gain[...]).astype(BF16)
        delta = jnp.dot(ow[...], normed, preferred_element_type=F32)
        out_ref[0, 0, :, pl.ds(j, tj)] = (
            own[0, 0, :, pl.ds(j, tj)].astype(F32) + delta
        ).astype(BF16)

    @pl.when(small)
    def _():
        @pl.loop(0, cols // tj)
        def _(step):
            j = pl.multiple_of(step * tj, tj)
            qb = qbuf[:, pl.ds(j, tj)]

            def scores(kc):
                return jnp.dot(kbuf[kc : kc + tk, :], qb, preferred_element_type=F32)

            total = None
            ahead = scores(0)
            for kc in range(0, keys, tk):
                s = ahead
                if kc + tk < keys:
                    ahead = scores(kc + tk)
                p = jnp.exp2(s * mult).astype(BF16)
                term = jnp.dot(vbuf[:, kc : kc + tk], p, preferred_element_type=F32)
                total = term if total is None else total + term
            finish(j, total)

    @pl.when(jnp.logical_not(small))
    def _():
        @pl.loop(0, cols // tj)
        def _(step):
            j = pl.multiple_of(step * tj, tj)
            qb = qbuf[:, pl.ds(j, tj)]

            def scores(i):
                kc = pl.multiple_of(i * tk, tk)
                return jnp.dot(kbuf[pl.ds(kc, tk), :], qb, preferred_element_type=F32) * scale

            peak = lax.fori_loop(
                0,
                keys // tk,
                lambda i, m: jnp.maximum(m, jnp.max(scores(i), axis=0, keepdims=True)),
                jnp.full((1, tj), -jnp.inf, F32),
            )
            acc[...] = jnp.zeros_like(acc)

            @pl.loop(0, keys // tk)
            def _(i):
                p = jnp.exp(scores(i) - peak).astype(BF16)
                kc = pl.multiple_of(i * tk, tk)
                acc[...] += jnp.dot(vbuf[:, pl.ds(kc, tk)], p, preferred_element_type=F32)

            finish(j, acc[...])


def attend_row(row, own, blocks, wkv, gain, ow, out_buf, out_shape):
    chan, cols = own.shape[2], own.shape[3]
    att = gain.shape[0]
    count = len(blocks)
    keys = count * cols
    tj, tk = min(1024, cols), 256

    def whole(a):
        return pl.BlockSpec(a.shape, lambda v: (0,) * a.ndim)

    return pl.pallas_call(
        functools.partial(attend_kernel, count, tj, tk),
        grid=(2,),
        in_specs=[pl.BlockSpec((1, 1, chan, cols), lambda v: (v, 0, 0, 0))]
        + [pl.BlockSpec((1, 1, chan, cols), lambda v: (1 - v, 0, 0, 0))] * count
        + [whole(wkv), whole(gain), whole(ow), pl.BlockSpec(memory_space=pl.ANY)],
        out_specs=[
            pl.BlockSpec((1, 1, chan, cols), lambda v: (v, row, 0, 0)),
            pl.BlockSpec((8, 128), lambda v: (0, 0)),
        ],
        out_shape=[
            jax.ShapeDtypeStruct(out_shape, BF16),
            jax.ShapeDtypeStruct((8, 128), F32),
        ],
        scratch_shapes=[
            pltpu.VMEM((keys, att), BF16),
            pltpu.VMEM((att + 16, keys), BF16),
            pltpu.VMEM((att, cols), BF16),
            pltpu.VMEM((att + 16, tj), F32),
        ],
        input_output_aliases={4 + count: 0},
        compiler_params=pltpu.CompilerParams(vmem_limit_bytes=VMEM_LIMIT),
        cost_estimate=pl.CostEstimate(
            flops=2 * 2 * 2 * 2 * cols * keys * att,
            bytes_accessed=2 * 2 * (count + 2) * chan * cols,
            transcendentals=2 * cols * keys,
        ),
        name="attend_row",
    )(own, *blocks, wkv, gain, ow, out_buf)


def body(views, conv_weight, match_weight, value_weight, post_gain, out_weight):
    _, rows, chan, cols = views.shape
    lat, lon = lax.axis_size("lat"), lax.axis_size("lon")
    forward = [(i, (i + 1) % lon) for i in range(lon)]
    backward = [((i + 1) % lon, i) for i in range(lon)]
    down = [(i, i + 1) for i in range(lat - 1)]
    up = [(i + 1, i) for i in range(lat - 1)]
    swap = [(i, i ^ 1) for i in range(lon)]

    last_row, first_row = lax.optimization_barrier((views[:, rows - 1 :], views[:, :1]))
    top = lax.ppermute(last_row, "lat", down)
    bottom = lax.ppermute(first_row, "lat", up)
    from_left = lax.ppermute(views[..., cols - 1], "lon", forward)
    from_right = lax.ppermute(views[..., 0], "lon", backward)
    edges = jnp.concatenate(
        [
            from_right[..., None],
            jnp.zeros((2, rows, chan, 126), BF16),
            from_left[..., None],
        ],
        axis=3,
    )
    edge_top = lax.ppermute(edges[:, rows - 1 :], "lat", down)
    edge_bottom = lax.ppermute(edges[:, :1], "lat", up)

    row_total = rows * lat
    row_index = (lax.axis_index("lat") * rows + jnp.arange(rows, dtype=jnp.int32)).astype(F32)
    latitude = (row_index + 0.5 - 0.5 * row_total) * (2.8 / row_total)
    side = 1.0 / (jnp.cos(latitude) + 0.25)
    wkv = jnp.concatenate([match_weight, value_weight], axis=0)
    gain = post_gain[:, None]

    def source(r, own, first, last):
        if r < 0:
            return (first, 0)
        if r >= rows:
            return (last, 0)
        return (own, r)

    def convolve(r, after):
        parts = [source(r + a, views, top, bottom) for a in (-1, 0, 1)]
        sides = [source(r + a, edges, edge_top, edge_bottom) for a in (-1, 0, 1)]
        return conv_row(r, side, parts, sides, conv_weight, after)

    def gather(own, after):
        far = [
            lax.ppermute(own, "lon", [(i, (i + 2 * s) % lon) for i in range(lon)])
            for s in range(1, lon // 2)
        ]
        near = [lax.ppermute(lax.optimization_barrier((own, after))[0], "lon", swap)]
        held = [lax.optimization_barrier((b, after))[0] for b in far]
        return [own] + far + near + [lax.ppermute(b, "lon", swap) for b in held]

    def attend(out, row):
        r, own, blocks = row
        return attend_row(r, own, blocks, wkv, gain, out_weight, out, views.shape)

    owns = []
    after = (last_row, first_row)
    order = list(range(1, rows - 1)) + [0, rows - 1]
    for r in order:
        if r == 0:
            after = lax.optimization_barrier((after[0], top, bottom))[:1]
        owns.append(convolve(r, after))
        after = (owns[-1],)
    out = jnp.zeros(views.shape, BF16)
    holds = [after, after]
    for i, (r, own) in enumerate(zip(order, owns)):
        out, token = attend(out, (r, own, gather(own, holds[i])))
        holds.append((token,))
    return out


def solution(mesh):
    placed = (P(None, "lat", None, "lon"), P(), P(), P(), P(), P())
    return jax.shard_map(
        body, mesh=mesh, in_specs=placed, out_specs=P(None, "lat", None, "lon"), check_vma=False
    )
```

time: 283 us -> 194 us (0.69)
  Pallas kernels: 223 us -> 142 us
  waiting for transfers between devices: 30 us -> 16.1 us
  local copies, waits for them, and re-layouts: 8.61 us -> 11.6 us
    pallas_call x4, Pallas kernels: 199 us -> 120 us  [attend_row(): pl.pallas_call(functools.partial(attend_kernel, count, tj, tk), grid=(2,)...]
    ppermute x1, waiting for transfers between devices: 23.9 us -> 2.08 us  [body(): edge_top = lax.ppermute(edges[:, rows - 1:], 'lat', down)]
    ppermute x14, waiting for transfers between devices: 3.57 us -> 14 us  [the longest x1 14 us: body(): top = lax.ppermute(last_row, 'lat', down)]
    ppermute x14, starting transfers between devices: 9.49 us -> 13.1 us  [the longest x1 5.45 us: body(): top = lax.ppermute(last_row, 'lat', down)]
  transfers between devices with their start and end apart: 18 -> 18, of which waited for: 5 -> 2; matrix products, arithmetic and copies ran while one was open for 2% -> 4% of each run, Pallas kernels for 59% -> 58%
where the time goes in v2:
time: 194 us; the launch traced here: 193 us
  Pallas kernels  142 us (73%)
  starting transfers between devices  20.4 us (11%)
  waiting for transfers between devices  16.1 us (8%)
  local copies, waits for them, and re-layouts  11.6 us (6%)
  other arithmetic  2.24 us (1%)
    pallas_call x4, Pallas kernels, attend_row(): pl.pallas_call(functools.partial(attend_kernel, count, tj, tk), grid=(2,)...  120 us
    pallas_call x4, Pallas kernels, conv_row(): pl.pallas_call(functools.partial(conv_kernel, row), grid=(2,), in_specs=[...  22 us
    ppermute x1, waiting for transfers between devices, body(): top = lax.ppermute(last_row, 'lat', down)  14 us
    ppermute x1, starting transfers between devices, body(): top = lax.ppermute(last_row, 'lat', down)  5.45 us
    unnamed x44, local copies, waits for them, and re-layouts  5 us
    ppermute x4, starting transfers between devices, gather(): lax.ppermute(own, 'lon', [(i, (i + 2 * s) % lon) for i in range(lon)])  4.11 us
  transfers between devices with their start and end apart: 18, of which 2 were waited for; matrix products, arithmetic and copies ran while one was open for 4% of the time, Pallas kernels for 58%

profile of v2, /device:TPU:0, one launch (start us, length us, event | category | flops | bytes accessed | tf_op | source)
XLA Modules:
  0.0 193.0 jit_solution(12964782335815150570)
XLA Ops:
  0.0 1.6 slice_reduce_fusion.1
  1.6 2.4 %collective-permute-start.1 = (bf16[2,4,192]{2,1,0:T(4,128)(2,1)S(1)}, bf16[2,4,192]{2,1,0:T(4,128)(2,1)S(1)}, u32[]{:S(2)}, u32[]{:S(2)}) collective-permute-start(bf16[2,4,192]{2,1,0:T(4,128)(2,1)S(1)} %get-tuple-element.39), channel_id=1, source_target_pairs={{1,0},{2,1},{3,2},{0,3},{5,4},{6,5},{7,6},{4,7},{9,8},{10,9},{11,1... | collective-permute-start | bytes 9224 | tf_op jit(solution)/shard_map/ppermute | solution.py:201
  4.0 1.5 fusion
  5.6 1.3 collective-permute-start
  6.9 5.4 %collective-permute-start.4 = (bf16[2,1,192,1024]{3,2,1,0:T(8,128)(2,1)S(1)}, bf16[2,1,192,1024]{3,2,1,0:T(8,128)(2,1)}, u32[]{:S(2)}, u32[]{:S(2)}) collective-permute-start(bf16[2,1,192,1024]{3,2,1,0:T(8,128)(2,1)S(1)} %get-tuple-element.23.refs_0_), channel_id=1, source_target_pairs={{0,4},{4,8},{8,12},{12,16},{16,20},{20,24},{24,28},{1,5},{5,9},{9,... | collective-permute-start | bytes 2359304 | tf_op jit(solution)/shard_map/ppermute | solution.py:198
  12.3 0.6 add_divide_fusion.side_ref
  13.5 1.0 pad_maximum_fusion.eu.em.ed
  14.5 5.5 %conv_row.4.refs_0_.refs_1_ = bf16[2,1,192,1024]{3,2,1,0:T(8,128)(2,1)} custom-call(f32[4]{0:T(128)} %add_divide_fusion.side_ref, bf16[2,4,192,1024]{3,2,1,0:T(8,128)(2,1)} %xm.7, bf16[2,4,192,1024]{3,2,1,0:T(8,128)(2,1)} %xm.7, bf16[2,4,192,1024]{3,2,1,0:T(8,128)(2,1)} %xm.7, bf16[2,4,192,128]{3,2,1,0:T(8,128)(2,1)} %pad_maximum_fusion.eu.em.ed, ...), custom_call_target="tpu_custom_call" | custom-call | flops 1358954496 | bytes 3145728 | tf_op jit(solution)/shard_map/conv_row/pallas_call | solution.py:41
  20.1 1.1 collective-permute-start.10
  21.1 3.5 %collective-permute-start.5 = (bf16[2,1,192,128]{3,2,1,0:T(8,128)(2,1)S(1)}, bf16[2,1,192,128]{3,2,1,0:T(8,128)(2,1)S(1)}, u32[]{:S(2)}, u32[]{:S(2)}) collective-permute-start(bf16[2,1,192,128]{3,2,1,0:T(8,128)(2,1)S(1)} %get-tuple-element.43), channel_id=1, source_target_pairs={{0,4},{4,8},{8,12},{12,16},{16,20},{20,24},{24,28},{1,5},{5,9},{9,... | collective-permute-start | bytes 294920 | tf_op jit(solution)/shard_map/ppermute | solution.py:210
  24.6 1.5 collective-permute-start.3
  26.1 5.5 %conv_row.5.refs_0_.refs_1_ = bf16[2,1,192,1024]{3,2,1,0:T(8,128)(2,1)} custom-call(f32[4]{0:T(128)} %add_divide_fusion.side_ref, bf16[2,4,192,1024]{3,2,1,0:T(8,128)(2,1)} %xm.7, bf16[2,4,192,1024]{3,2,1,0:T(8,128)(2,1)} %xm.7, bf16[2,4,192,1024]{3,2,1,0:T(8,128)(2,1)} %xm.7, bf16[2,4,192,128]{3,2,1,0:T(8,128)(2,1)} %pad_maximum_fusion.eu.em.ed, ...), custom_call_target="tpu_custom_call" | custom-call | flops 1358954496 | bytes 3145728 | tf_op jit(solution)/shard_map/conv_row/pallas_call | solution.py:41
  31.6 1.0 collective-permute-start.7
  32.6 14.0 %collective-permute-done.4.xu = bf16[2,1,192,1024]{3,2,1,0:T(8,128)(2,1)} collective-permute-done((bf16[2,1,192,1024]{3,2,1,0:T(8,128)(2,1)S(1)}, bf16[2,1,192,1024]{3,2,1,0:T(8,128)(2,1)}, u32[]{:S(2)}, u32[]{:S(2)}) %collective-permute-start.4) | collective-permute-done | bytes 786464 | tf_op jit(solution)/shard_map/ppermute | solution.py:198
  46.6 2.1 %collective-permute-done.5.eu = bf16[2,1,192,128]{3,2,1,0:T(8,128)(2,1)S(1)} collective-permute-done((bf16[2,1,192,128]{3,2,1,0:T(8,128)(2,1)S(1)}, bf16[2,1,192,128]{3,2,1,0:T(8,128)(2,1)S(1)}, u32[]{:S(2)}, u32[]{:S(2)}) %collective-permute-start.5) | collective-permute-done | bytes 98336 | tf_op jit(solution)/shard_map/ppermute | solution.py:210
  48.7 0.6 copy-done.9
  49.3 5.5 %conv_row.6.refs_0_.refs_1_ = bf16[2,1,192,1024]{3,2,1,0:T(8,128)(2,1)} custom-call(f32[4]{0:T(128)} %add_divide_fusion.side_ref, bf16[2,1,192,1024]{3,2,1,0:T(8,128)(2,1)} %collective-permute-done.4.xu, bf16[2,4,192,1024]{3,2,1,0:T(8,128)(2,1)} %xm.7, bf16[2,4,192,1024]{3,2,1,0:T(8,128)(2,1)} %xm.7, bf16[2,1,192,128]{3,2,1,0:T(8,128)(2,1)} %copy-done.9, ...), custom_call_target="tpu_custom_call" | custom-call | flops 1358954496 | bytes 3145728 | tf_op jit(solution)/shard_map/conv_row/pallas_call | solution.py:41
  54.9 0.6 copy-done.8
  55.5 5.5 %conv_row.7.refs_0_.refs_1_ = bf16[2,1,192,1024]{3,2,1,0:T(8,128)(2,1)} custom-call(f32[4]{0:T(128)} %add_divide_fusion.side_ref, bf16[2,4,192,1024]{3,2,1,0:T(8,128)(2,1)} %xm.7, bf16[2,4,192,1024]{3,2,1,0:T(8,128)(2,1)} %xm.7, bf16[2,1,192,1024]{3,2,1,0:T(8,128)(2,1)} %copy-done.7, bf16[2,4,192,128]{3,2,1,0:T(8,128)(2,1)} %pad_maximum_fusion.eu.em.ed, ...), custom_call_target="tpu_custom_call" | custom-call | flops 1358954496 | bytes 3145728 | tf_op jit(solution)/shard_map/conv_row/pallas_call | solution.py:41
  61.9 0.7 copy.32.refs_6_
  62.6 0.7 pad_maximum_fusion.1.refs_5_
  63.3 1.3 collective-permute-start.15
  64.6 0.7 collective-permute-start.6
  65.3 0.5 collective-permute-start.9
  65.8 2.1 %broadcast_in_dim.19.refs_8_ = bf16[2,4,192,1024]{3,2,1,0:T(8,128)(2,1)} broadcast(bf16[]{:T(256)} %constant.21.clone.1), dimensions={} | broadcast | bytes 3145730 | tf_op jit(solution)/shard_map/broadcast_in_dim | solution.py:253
  67.9 30.0 %attend_row.4 = (bf16[2,4,192,1024]{3,2,1,0:T(8,128)(2,1)}, f32[8,128]{1,0:T(8,128)}) custom-call(bf16[2,1,192,1024]{3,2,1,0:T(8,128)(2,1)} %conv_row.4.refs_0_.refs_1_, bf16[2,1,192,1024]{3,2,1,0:T(8,128)(2,1)} %conv_row.4.refs_0_.refs_1_, bf16[2,1,192,1024]{3,2,1,0:T(8,128)(2,1)} %collective-permute-done.10.refs_2_, ...), custom_call_target="tpu_custom_call", output_to_operand_aliasing={{0}: (8, {})} | custom-call | flops 8589934592 | bytes 4718592 | tf_op jit(solution)/shard_map/attend_row/pallas_call | solution.py:157
  98.5 0.9 copy-done.15
  99.7 30.3 %attend_row.5 = (bf16[2,4,192,1024]{3,2,1,0:T(8,128)(2,1)}, f32[8,128]{1,0:T(8,128)}) custom-call(bf16[2,1,192,1024]{3,2,1,0:T(8,128)(2,1)} %conv_row.5.refs_0_.refs_1_, bf16[2,1,192,1024]{3,2,1,0:T(8,128)(2,1)} %conv_row.5.refs_0_.refs_1_, bf16[2,1,192,1024]{3,2,1,0:T(8,128)(2,1)} %collective-permute-done.7.refs_2_, ...), custom_call_target="tpu_custom_call", output_to_operand_aliasing={{0}: (8, {})} | custom-call | flops 8589934592 | bytes 4718592 | tf_op jit(solution)/shard_map/attend_row/pallas_call | solution.py:157
  130.6 0.9 copy-done.16
  131.7 30.0 %attend_row.6 = (bf16[2,4,192,1024]{3,2,1,0:T(8,128)(2,1)}, f32[8,128]{1,0:T(8,128)}) custom-call(bf16[2,1,192,1024]{3,2,1,0:T(8,128)(2,1)} %conv_row.6.refs_0_.refs_1_, bf16[2,1,192,1024]{3,2,1,0:T(8,128)(2,1)} %conv_row.6.refs_0_.refs_1_, bf16[2,1,192,1024]{3,2,1,0:T(8,128)(2,1)} %copy-done.14, ...), custom_call_target="tpu_custom_call", output_to_operand_aliasing={{0}: (8, {})} | custom-call | flops 8589934592 | bytes 4718592 | tf_op jit(solution)/shard_map/attend_row/pallas_call | solution.py:157
  161.8 0.9 copy-done.19
  162.9 30.1 %attend_row.7 = (bf16[2,4,192,1024]{3,2,1,0:T(8,128)(2,1)}, f32[8,128]{1,0:T(8,128)}) custom-call(bf16[2,1,192,1024]{3,2,1,0:T(8,128)(2,1)} %conv_row.7.refs_0_.refs_1_, bf16[2,1,192,1024]{3,2,1,0:T(8,128)(2,1)} %conv_row.7.refs_0_.refs_1_, bf16[2,1,192,1024]{3,2,1,0:T(8,128)(2,1)} %copy-done.13, ...), custom_call_target="tpu_custom_call", output_to_operand_aliasing={{0}: (8, {})} | custom-call | flops 8589934592 | bytes 4718592 | tf_op jit(solution)/shard_map/attend_row/pallas_call | solution.py:157
  (68 shorter events, 3.6 us)
Async XLA Ops:
  1.6 11.3 %collective-permute-start.1 = (bf16[2,4,192]{2,1,0:T(4,128)(2,1)S(1)}, bf16[2,4,192]{2,1,0:T(4,128)(2,1)S(1)}, u32[]{:S(2)}, u32[]{:S(2)}) collective-permute-start(bf16[2,4,192]{2,1,0:T(4,128)(2,1)S(1)} %get-tuple-element.39), channel_id=1, source_target_pairs={{1,0},{2,1},{3,2},{0,3},{5,4},{6,5},{7,6},{4,7},{9,8},{10,9},{11,1... | collective-permute-start | bytes 9224 | tf_op jit(solution)/shard_map/ppermute | solution.py:201
  4.0 9.2 %collective-permute-start.2 = (bf16[2,4,192]{2,1,0:T(4,128)(2,1)S(1)}, bf16[2,4,192]{2,1,0:T(4,128)(2,1)S(1)}, u32[]{:S(2)}, u32[]{:S(2)}) collective-permute-start(bf16[2,4,192]{2,1,0:T(4,128)(2,1)S(1)} %get-tuple-element.40), channel_id=1, source_target_pairs={{0,1},{1,2},{2,3},{3,0},{4,5},{5,6},{6,7},{7,4},{8,9},{9,10},{10,1... | collective-permute-start | bytes 9224 | tf_op jit(solution)/shard_map/ppermute | solution.py:200
  5.5 9.0 %copy-start.3 = (bf16[2,1,192,1024]{3,2,1,0:T(8,128)(2,1)}, bf16[2,1,192,1024]{3,2,1,0:T(8,128)(2,1)S(1)}, u32[]{:S(2)}) copy-start(bf16[2,1,192,1024]{3,2,1,0:T(8,128)(2,1)S(1)} %get-tuple-element.23.refs_0_) | copy-start | bytes 2359300
  5.5 9.0 %copy-start.4 = (bf16[2,1,192,1024]{3,2,1,0:T(8,128)(2,1)}, bf16[2,1,192,1024]{3,2,1,0:T(8,128)(2,1)S(1)}, u32[]{:S(2)}) copy-start(bf16[2,1,192,1024]{3,2,1,0:T(8,128)(2,1)S(1)} %get-tuple-element.22.refs_1_) | copy-start | bytes 2359300
  5.6 26.0 %collective-permute-start = (bf16[2,1,192,1024]{3,2,1,0:T(8,128)(2,1)S(1)}, bf16[2,1,192,1024]{3,2,1,0:T(8,128)(2,1)S(1)}, u32[]{:S(2)}, u32[]{:S(2)}) collective-permute-start(bf16[2,1,192,1024]{3,2,1,0:T(8,128)(2,1)S(1)} %get-tuple-element.22.refs_1_), channel_id=1, source_target_pairs={{4,0},{8,4},{12,8},{16,12},{20,16},{24,20},{28,24},{5,1},{9,5},{13... | collective-permute-start | bytes 2359304 | tf_op jit(solution)/shard_map/ppermute | solution.py:199
  6.9 39.7 %collective-permute-start.4 = (bf16[2,1,192,1024]{3,2,1,0:T(8,128)(2,1)S(1)}, bf16[2,1,192,1024]{3,2,1,0:T(8,128)(2,1)}, u32[]{:S(2)}, u32[]{:S(2)}) collective-permute-start(bf16[2,1,192,1024]{3,2,1,0:T(8,128)(2,1)S(1)} %get-tuple-element.23.refs_0_), channel_id=1, source_target_pairs={{0,4},{4,8},{8,12},{12,16},{16,20},{20,24},{24,28},{1,5},{5,9},{9,... | collective-permute-start | bytes 2359304 | tf_op jit(solution)/shard_map/ppermute | solution.py:198
  14.5 6.6 %copy-start = (bf16[2,4,192,128]{3,2,1,0:T(8,128)(2,1)S(1)}, bf16[2,4,192,128]{3,2,1,0:T(8,128)(2,1)}, u32[]{:S(2)}) copy-start(bf16[2,4,192,128]{3,2,1,0:T(8,128)(2,1)} %pad_maximum_fusion.eu.em.ed) | copy-start | bytes 1179652
  20.1 41.1 %collective-permute-start.10 = (bf16[2,1,192,1024]{3,2,1,0:T(8,128)(2,1)}, bf16[2,1,192,1024]{3,2,1,0:T(8,128)(2,1)}, u32[]{:S(2)}, u32[]{:S(2)}) collective-permute-start(bf16[2,1,192,1024]{3,2,1,0:T(8,128)(2,1)} %conv_row.4.refs_0_.refs_1_), channel_id=1, source_target_pairs={{0,2},{1,3},{2,0},{3,1},{4,6},{5,7},{6,4},{7,5},{8,10},{9,11},{10,... | collective-permute-start | bytes 2359304 | tf_op jit(solution)/shard_map/ppermute | solution.py:234
  21.1 27.5 %collective-permute-start.5 = (bf16[2,1,192,128]{3,2,1,0:T(8,128)(2,1)S(1)}, bf16[2,1,192,128]{3,2,1,0:T(8,128)(2,1)S(1)}, u32[]{:S(2)}, u32[]{:S(2)}) collective-permute-start(bf16[2,1,192,128]{3,2,1,0:T(8,128)(2,1)S(1)} %get-tuple-element.43), channel_id=1, source_target_pairs={{0,4},{4,8},{8,12},{12,16},{16,20},{20,24},{24,28},{1,5},{5,9},{9,... | collective-permute-start | bytes 294920 | tf_op jit(solution)/shard_map/ppermute | solution.py:210
  24.6 30.3 %collective-permute-start.3 = (bf16[2,1,192,128]{3,2,1,0:T(8,128)(2,1)S(1)}, bf16[2,1,192,128]{3,2,1,0:T(8,128)(2,1)S(1)}, u32[]{:S(2)}, u32[]{:S(2)}) collective-permute-start(bf16[2,1,192,128]{3,2,1,0:T(8,128)(2,1)S(1)} %get-tuple-element.44), channel_id=1, source_target_pairs={{4,0},{8,4},{12,8},{16,12},{20,16},{24,20},{28,24},{5,1},{9,5},{13... | collective-permute-start | bytes 294920 | tf_op jit(solution)/shard_map/ppermute | solution.py:211
  31.6 23.2 %copy-start.7 = (bf16[2,1,192,1024]{3,2,1,0:T(8,128)(2,1)}, bf16[2,1,192,1024]{3,2,1,0:T(8,128)(2,1)S(1)}, u32[]{:S(2)}) copy-start(bf16[2,1,192,1024]{3,2,1,0:T(8,128)(2,1)S(1)} %collective-permute-done.xd) | copy-start | bytes 2359300
  31.6 33.7 %collective-permute-start.7 = (bf16[2,1,192,1024]{3,2,1,0:T(8,128)(2,1)}, bf16[2,1,192,1024]{3,2,1,0:T(8,128)(2,1)}, u32[]{:S(2)}, u32[]{:S(2)}) collective-permute-start(bf16[2,1,192,1024]{3,2,1,0:T(8,128)(2,1)} %conv_row.5.refs_0_.refs_1_), channel_id=1, source_target_pairs={{0,2},{1,3},{2,0},{3,1},{4,6},{5,7},{6,4},{7,5},{8,10},{9,11},{10,... | collective-permute-start | bytes 2359304 | tf_op jit(solution)/shard_map/ppermute | solution.py:234
  54.8 6.2 %copy-start.2 = (bf16[2,1,192,1024]{3,2,1,0:T(8,128)(2,1)S(1)}, bf16[2,1,192,1024]{3,2,1,0:T(8,128)(2,1)}, u32[]{:S(2)}) copy-start(bf16[2,1,192,1024]{3,2,1,0:T(8,128)(2,1)} %conv_row.4.refs_0_.refs_1_) | copy-start | bytes 2359300
  54.8 6.8 %copy-start.10 = (bf16[128,192]{0,1:T(8,128)(2,1)S(1)}, bf16[128,192]{0,1:T(8,128)(2,1)}, u32[]{:S(2)}) copy-start(bf16[128,192]{0,1:T(8,128)(2,1)} %param.8) | copy-start | bytes 147460
  54.8 6.9 %copy-start.11 = (bf16[128,192]{0,1:T(8,128)(2,1)S(1)}, bf16[128,192]{0,1:T(8,128)(2,1)}, u32[]{:S(2)}) copy-start(bf16[128,192]{0,1:T(8,128)(2,1)} %param.9) | copy-start | bytes 147460
  54.8 7.0 %copy-start.12 = (f32[128]{0:T(128)S(1)}, f32[128]{0:T(128)}, u32[]{:S(2)}) copy-start(f32[128]{0:T(128)} %param.10) | copy-start | bytes 1540
  54.8 8.4 %copy-start.5 = (bf16[2,1,192,1024]{3,2,1,0:T(8,128)(2,1)S(1)}, bf16[2,1,192,1024]{3,2,1,0:T(8,128)(2,1)}, u32[]{:S(2)}) copy-start(bf16[2,1,192,1024]{3,2,1,0:T(8,128)(2,1)} %conv_row.6.refs_0_.refs_1_) | copy-start | bytes 2359300
  54.8 10.5 %copy-start.1 = (bf16[2,1,192,1024]{3,2,1,0:T(8,128)(2,1)S(1)}, bf16[2,1,192,1024]{3,2,1,0:T(8,128)(2,1)}, u32[]{:S(2)}) copy-start(bf16[2,1,192,1024]{3,2,1,0:T(8,128)(2,1)} %conv_row.5.refs_0_.refs_1_) | copy-start | bytes 2359300
  61.0 4.3 %collective-permute-start.11 = (bf16[2,1,192,1024]{3,2,1,0:T(8,128)(2,1)S(1)}, bf16[2,1,192,1024]{3,2,1,0:T(8,128)(2,1)}, u32[]{:S(2)}, u32[]{:S(2)}) collective-permute-start(bf16[2,1,192,1024]{3,2,1,0:T(8,128)(2,1)S(1)} %copy-done.2), channel_id=1, source_target_pairs={{0,1},{1,0},{2,3},{3,2},{4,5},{5,4},{6,7},{7,6},{8,9},{9,8},{10,11... | collective-permute-start | bytes 2359304 | tf_op jit(solution)/shard_map/ppermute | solution.py:237
  61.1 4.7 %collective-permute-start.12 = (bf16[2,1,192,1024]{3,2,1,0:T(8,128)(2,1)}, bf16[2,1,192,1024]{3,2,1,0:T(8,128)(2,1)}, u32[]{:S(2)}, u32[]{:S(2)}) collective-permute-start(bf16[2,1,192,1024]{3,2,1,0:T(8,128)(2,1)} %collective-permute-done.10.refs_2_), channel_id=1, source_target_pairs={{0,1},{1,0},{2,3},{3,2},{4,5},{5,4},{6,7},{7,6},{8,9},{9,8},{10,11... | collective-permute-start | bytes 2359304 | tf_op jit(solution)/shard_map/ppermute | solution.py:239
  63.3 34.7 %collective-permute-start.15 = (bf16[2,1,192,1024]{3,2,1,0:T(8,128)(2,1)S(1)}, bf16[2,1,192,1024]{3,2,1,0:T(8,128)(2,1)S(1)}, u32[]{:S(2)}, u32[]{:S(2)}) collective-permute-start(bf16[2,1,192,1024]{3,2,1,0:T(8,128)(2,1)S(1)} %copy-done.5), channel_id=1, source_target_pairs={{0,2},{1,3},{2,0},{3,1},{4,6},{5,7},{6,4},{7,5},{8,10},{9,11},{10,... | collective-permute-start | bytes 2359304 | tf_op jit(solution)/shard_map/ppermute | solution.py:234
  64.6 65.4 %collective-permute-start.6 = (bf16[2,1,192,1024]{3,2,1,0:T(8,128)(2,1)}, bf16[2,1,192,1024]{3,2,1,0:T(8,128)(2,1)S(1)}, u32[]{:S(2)}, u32[]{:S(2)}) collective-permute-start(bf16[2,1,192,1024]{3,2,1,0:T(8,128)(2,1)} %conv_row.7.refs_0_.refs_1_), channel_id=1, source_target_pairs={{0,2},{1,3},{2,0},{3,1},{4,6},{5,7},{6,4},{7,5},{8,10},{9,11},{10,... | collective-permute-start | bytes 2359304 | tf_op jit(solution)/shard_map/ppermute | solution.py:234
  65.3 33.2 %collective-permute-start.8 = (bf16[2,1,192,1024]{3,2,1,0:T(8,128)(2,1)S(1)}, bf16[2,1,192,1024]{3,2,1,0:T(8,128)(2,1)S(1)}, u32[]{:S(2)}, u32[]{:S(2)}) collective-permute-start(bf16[2,1,192,1024]{3,2,1,0:T(8,128)(2,1)S(1)} %copy-done.1), channel_id=1, source_target_pairs={{0,1},{1,0},{2,3},{3,2},{4,5},{5,4},{6,7},{7,6},{8,9},{9,8},{10,11... | collective-permute-start | bytes 2359304 | tf_op jit(solution)/shard_map/ppermute | solution.py:237
  65.3 33.2 %collective-permute-start.9 = (bf16[2,1,192,1024]{3,2,1,0:T(8,128)(2,1)}, bf16[2,1,192,1024]{3,2,1,0:T(8,128)(2,1)S(1)}, u32[]{:S(2)}, u32[]{:S(2)}) collective-permute-start(bf16[2,1,192,1024]{3,2,1,0:T(8,128)(2,1)} %collective-permute-done.7.refs_2_), channel_id=1, source_target_pairs={{0,1},{1,0},{2,3},{3,2},{4,5},{5,4},{6,7},{7,6},{8,9},{9,8},{10,11... | collective-permute-start | bytes 2359304 | tf_op jit(solution)/shard_map/ppermute | solution.py:239
  97.9 32.1 %copy-start.14 = (bf16[2,1,192,1024]{3,2,1,0:T(8,128)(2,1)}, bf16[2,1,192,1024]{3,2,1,0:T(8,128)(2,1)S(1)}, u32[]{:S(2)}) copy-start(bf16[2,1,192,1024]{3,2,1,0:T(8,128)(2,1)S(1)} %collective-permute-done.15.refs_2_) | copy-start | bytes 2359300
  97.9 32.6 %collective-permute-start.17 = (bf16[2,1,192,1024]{3,2,1,0:T(8,128)(2,1)S(1)}, bf16[2,1,192,1024]{3,2,1,0:T(8,128)(2,1)S(1)}, u32[]{:S(2)}, u32[]{:S(2)}) collective-permute-start(bf16[2,1,192,1024]{3,2,1,0:T(8,128)(2,1)S(1)} %collective-permute-done.15.refs_2_), channel_id=1, source_target_pairs={{0,1},{1,0},{2,3},{3,2},{4,5},{5,4},{6,7},{7,6},{8,9},{9,8},{10,11... | collective-permute-start | bytes 2359304 | tf_op jit(solution)/shard_map/ppermute | solution.py:239
  98.1 32.5 %collective-permute-start.16 = (bf16[2,1,192,1024]{3,2,1,0:T(8,128)(2,1)S(1)}, bf16[2,1,192,1024]{3,2,1,0:T(8,128)(2,1)S(1)}, u32[]{:S(2)}, u32[]{:S(2)}) collective-permute-start(bf16[2,1,192,1024]{3,2,1,0:T(8,128)(2,1)S(1)} %copy-done.5), channel_id=1, source_target_pairs={{0,1},{1,0},{2,3},{3,2},{4,5},{5,4},{6,7},{7,6},{8,9},{9,8},{10,11... | collective-permute-start | bytes 2359304 | tf_op jit(solution)/shard_map/ppermute | solution.py:237
  98.5 1.2 copy-start.18
  99.7 30.4 %copy-start.6 = (bf16[2,1,192,1024]{3,2,1,0:T(8,128)(2,1)S(1)}, bf16[2,1,192,1024]{3,2,1,0:T(8,128)(2,1)}, u32[]{:S(2)}) copy-start(bf16[2,1,192,1024]{3,2,1,0:T(8,128)(2,1)} %conv_row.7.refs_0_.refs_1_) | copy-start | bytes 2359300
  130.0 31.8 %copy-start.13 = (bf16[2,1,192,1024]{3,2,1,0:T(8,128)(2,1)}, bf16[2,1,192,1024]{3,2,1,0:T(8,128)(2,1)S(1)}, u32[]{:S(2)}) copy-start(bf16[2,1,192,1024]{3,2,1,0:T(8,128)(2,1)S(1)} %collective-permute-done.6.refs_2_) | copy-start | bytes 2359300
  130.0 31.8 %collective-permute-start.14 = (bf16[2,1,192,1024]{3,2,1,0:T(8,128)(2,1)S(1)}, bf16[2,1,192,1024]{3,2,1,0:T(8,128)(2,1)S(1)}, u32[]{:S(2)}, u32[]{:S(2)}) collective-permute-start(bf16[2,1,192,1024]{3,2,1,0:T(8,128)(2,1)S(1)} %collective-permute-done.6.refs_2_), channel_id=1, source_target_pairs={{0,1},{1,0},{2,3},{3,2},{4,5},{5,4},{6,7},{7,6},{8,9},{9,8},{10,11... | collective-permute-start | bytes 2359304 | tf_op jit(solution)/shard_map/ppermute | solution.py:239
  130.1 31.7 %collective-permute-start.13 = (bf16[2,1,192,1024]{3,2,1,0:T(8,128)(2,1)S(1)}, bf16[2,1,192,1024]{3,2,1,0:T(8,128)(2,1)S(1)}, u32[]{:S(2)}, u32[]{:S(2)}) collective-permute-start(bf16[2,1,192,1024]{3,2,1,0:T(8,128)(2,1)S(1)} %copy-done.6), channel_id=1, source_target_pairs={{0,1},{1,0},{2,3},{3,2},{4,5},{5,4},{6,7},{7,6},{8,9},{9,8},{10,11... | collective-permute-start | bytes 2359304 | tf_op jit(solution)/shard_map/ppermute | solution.py:237
  (7 other events, 6.2 us)

commit v3 on v2

--- a/solution.py
+++ b/solution.py
@@ -62,7 +62,7 @@
     own = refs[0]
     blocks = refs[1 : 1 + count]
     wkv, gain, ow = refs[1 + count : 4 + count]
-    out_ref, token, kbuf, vbuf, qbuf, acc = refs[5 + count :]
+    out_ref, token, kbuf, vbuf, qbuf, acc = refs[-6:]
     chan = wkv.shape[0] // 2
     cols = own.shape[3]
     keys = kbuf.shape[0]
@@ -159,7 +159,8 @@
         grid=(2,),
         in_specs=[pl.BlockSpec((1, 1, chan, cols), lambda v: (v, 0, 0, 0))]
         + [pl.BlockSpec((1, 1, chan, cols), lambda v: (1 - v, 0, 0, 0))] * count
-        + [whole(wkv), whole(gain), whole(ow), pl.BlockSpec(memory_space=pl.ANY)],
+        + [whole(wkv), whole(gain), whole(ow)]
+        + [pl.BlockSpec(memory_space=pl.ANY) for _ in out_buf],
         out_specs=[
             pl.BlockSpec((1, 1, chan, cols), lambda v: (v, row, 0, 0)),
             pl.BlockSpec((8, 128), lambda v: (0, 0)),
@@ -174,7 +175,7 @@
             pltpu.VMEM((att, cols), BF16),
             pltpu.VMEM((att + 16, tj), F32),
         ],
-        input_output_aliases={4 + count: 0},
+        input_output_aliases={4 + count: 0} if out_buf else {},
         compiler_params=pltpu.CompilerParams(vmem_limit_bytes=VMEM_LIMIT),
         cost_estimate=pl.CostEstimate(
             flops=2 * 2 * 2 * 2 * cols * keys * att,
@@ -182,7 +183,7 @@
             transcendentals=2 * cols * keys,
         ),
         name="attend_row",
-    )(own, *blocks, wkv, gain, ow, out_buf)
+    )(own, *blocks, wkv, gain, ow, *out_buf)
 
 
 def body(views, conv_weight, match_weight, value_weight, post_gain, out_weight):
@@ -245,17 +246,18 @@
     owns = []
     after = (last_row, first_row)
     order = list(range(1, rows - 1)) + [0, rows - 1]
-    for r in order:
-        if r == 0:
-            after = lax.optimization_barrier((after[0], top, bottom))[:1]
+    for r in order[:-2]:
         owns.append(convolve(r, after))
         after = (owns[-1],)
-    out = jnp.zeros(views.shape, BF16)
-    holds = [after, after]
-    for i, (r, own) in enumerate(zip(order, owns)):
-        out, token = attend(out, (r, own, gather(own, holds[i])))
-        holds.append((token,))
-    return out
+    whole, token = attend((), (order[0], owns[0], gather(owns[0], after + (bottom,))))
+    after = (token,)
+    for r in order[-2:]:
+        owns.append(convolve(r, after))
+        after = (owns[-1],)
+    for r, own in list(zip(order, owns))[1:]:
+        whole, token = attend((whole,), (r, own, gather(own, after)))
+        after = (token,)
+    return whole
 
 
 def solution(mesh):

time: 194 us -> 200 us (1.031)
  waiting for transfers between devices: 16.1 us -> 21.4 us
    ppermute x1, waiting for transfers between devices: 14 us -> 0.01 us  [body(): top = lax.ppermute(last_row, 'lat', down)]
    ppermute x4, waiting for transfers between devices: 0.01 us -> 7.58 us  [gather(): lax.ppermute(own, 'lon', [(i, (i + 2 * s) % lon) for i in range(lon)])]
    ppermute x1, waiting for transfers between devices: 0.01 us -> 6.38 us  [body(): bottom = lax.ppermute(first_row, 'lat', up)]
    ppermute x4, waiting for transfers between devices: 0.01 us -> 4.07 us  [gather(): lax.ppermute(lax.optimization_barrier((own, after))[0], 'lon', swap)]
    ppermute x4, waiting for transfers between devices: 0.01 us -> 3.37 us  [gather(): return [own] + far + near + [lax.ppermute(b, 'lon', swap) for b in held]]
    unnamed x44, local copies, waits for them, and re-layouts: 5 us -> 7.3 us
    ppermute x1, waiting for transfers between devices: 2.08 us -> 0.01 us  [body(): edge_top = lax.ppermute(edges[:, rows - 1:], 'lat', down)]
    broadcast_in_dim x1 -> x0, local copies, waits for them, and re-layouts: 2.06 us -> none  [body(): out = jnp.zeros(views.shape, BF16)]
  transfers between devices with their start and end apart: 18 -> 18, of which waited for: 2 -> 8; matrix products, arithmetic and copies ran while one was open for 4% -> 5% of each run, Pallas kernels for 58% -> 56%
where the time goes in v3:
time: 200 us; the launch traced here: 199 us
  Pallas kernels  142 us (71%)
  waiting for transfers between devices  21.4 us (11%)
  starting transfers between devices  19.2 us (10%)
  local copies, waits for them, and re-layouts  12.7 us (6%)
  other arithmetic  3.15 us (2%)
    pallas_call x4, Pallas kernels, attend_row(): pl.pallas_call(functools.partial(attend_kernel, count, tj, tk), grid=(2,)...  120 us
    pallas_call x4, Pallas kernels, conv_row(): pl.pallas_call(functools.partial(conv_kernel, row), grid=(2,), in_specs=[...  21.9 us
    ppermute x4, waiting for transfers between devices, gather(): lax.ppermute(own, 'lon', [(i, (i + 2 * s) % lon) for i in range(lon)])  7.58 us
    unnamed x44, local copies, waits for them, and re-layouts  7.3 us
    ppermute x1, waiting for transfers between devices, body(): bottom = lax.ppermute(first_row, 'lat', up)  6.38 us
    ppermute x1, starting transfers between devices, body(): top = lax.ppermute(last_row, 'lat', down)  4.31 us
    ppermute x1, starting transfers between devices, body(): edge_top = lax.ppermute(edges[:, rows - 1:], 'lat', down)  4.28 us
    ppermute x4, waiting for transfers between devices, gather(): lax.ppermute(lax.optimization_barrier((own, after))[0], 'lon', swap)  4.07 us
  transfers between devices with their start and end apart: 18, of which 8 were waited for; matrix products, arithmetic and copies ran while one was open for 5% of the time, Pallas kernels for 56%

profile of v3, /device:TPU:0, one launch (start us, length us, event | category | flops | bytes accessed | tf_op | source)
XLA Modules:
  0.0 199.1 jit_solution(15251501612242981758)
XLA Ops:
  0.0 1.6 slice_reduce_fusion.1
  1.6 2.4 %collective-permute-start.1 = (bf16[2,4,192]{2,1,0:T(4,128)(2,1)S(1)}, bf16[2,4,192]{2,1,0:T(4,128)(2,1)S(1)}, u32[]{:S(2)}, u32[]{:S(2)}) collective-permute-start(bf16[2,4,192]{2,1,0:T(4,128)(2,1)S(1)} %get-tuple-element.39), channel_id=1, source_target_pairs={{1,0},{2,1},{3,2},{0,3},{5,4},{6,5},{7,6},{4,7},{9,8},{10,9},{11,1... | collective-permute-start | bytes 9224 | tf_op jit(solution)/shard_map/ppermute | solution.py:202
  4.0 2.4 %fusion = (bf16[2,1,192,1024]{3,2,1,0:T(8,128)(2,1)S(1)}, bf16[2,1,192,1024]{3,2,1,0:T(8,128)(2,1)}) fusion(bf16[2,4,192,1024]{3,2,1,0:T(8,128)(2,1)} %xm.7), kind=kLoop, calls=%fused_computation.5 | loop fusion | bytes 3145728 | tf_op jit(solution)/shard_map/slice | solution.py:198
  6.5 1.3 collective-permute-start
  9.0 1.0 pad_maximum_fusion.eu.em.ed
  10.0 5.5 %conv_row.4.refs_0_.refs_1_ = bf16[2,1,192,1024]{3,2,1,0:T(8,128)(2,1)} custom-call(f32[4]{0:T(128)} %add_divide_fusion.side_ref, bf16[2,4,192,1024]{3,2,1,0:T(8,128)(2,1)} %xm.7, bf16[2,4,192,1024]{3,2,1,0:T(8,128)(2,1)} %xm.7, bf16[2,4,192,1024]{3,2,1,0:T(8,128)(2,1)} %xm.7, bf16[2,4,192,128]{3,2,1,0:T(8,128)(2,1)} %pad_maximum_fusion.eu.em.ed, ...), custom_call_target="tpu_custom_call" | custom-call | flops 1358954496 | bytes 3145728 | tf_op jit(solution)/shard_map/conv_row/pallas_call | solution.py:41
  15.6 1.1 collective-permute-start.6
  16.7 5.5 %conv_row.5.refs_0_.refs_1_ = bf16[2,1,192,1024]{3,2,1,0:T(8,128)(2,1)} custom-call(f32[4]{0:T(128)} %add_divide_fusion.side_ref, bf16[2,4,192,1024]{3,2,1,0:T(8,128)(2,1)} %xm.7, bf16[2,4,192,1024]{3,2,1,0:T(8,128)(2,1)} %xm.7, bf16[2,4,192,1024]{3,2,1,0:T(8,128)(2,1)} %xm.7, bf16[2,4,192,128]{3,2,1,0:T(8,128)(2,1)} %pad_maximum_fusion.eu.em.ed, ...), custom_call_target="tpu_custom_call" | custom-call | flops 1358954496 | bytes 3145728 | tf_op jit(solution)/shard_map/conv_row/pallas_call | solution.py:41
  22.2 6.4 %collective-permute-done.xd = bf16[2,1,192,1024]{3,2,1,0:T(8,128)(2,1)S(1)} collective-permute-done((bf16[2,1,192,1024]{3,2,1,0:T(8,128)(2,1)S(1)}, bf16[2,1,192,1024]{3,2,1,0:T(8,128)(2,1)S(1)}, u32[]{:S(2)}, u32[]{:S(2)}) %collective-permute-start) | collective-permute-done | bytes 786464 | tf_op jit(solution)/shard_map/ppermute | solution.py:200
  28.5 7.6 %collective-permute-done.6.refs_2_ = bf16[2,1,192,1024]{3,2,1,0:T(8,128)(2,1)} collective-permute-done((bf16[2,1,192,1024]{3,2,1,0:T(8,128)(2,1)}, bf16[2,1,192,1024]{3,2,1,0:T(8,128)(2,1)}, u32[]{:S(2)}, u32[]{:S(2)}) %collective-permute-start.6) | collective-permute-done | bytes 786464 | tf_op jit(solution)/shard_map/ppermute | solution.py:235
  36.1 4.3 %collective-permute-start.4 = (bf16[2,1,192,1024]{3,2,1,0:T(8,128)(2,1)S(1)}, bf16[2,1,192,1024]{3,2,1,0:T(8,128)(2,1)S(1)}, u32[]{:S(2)}, u32[]{:S(2)}) collective-permute-start(bf16[2,1,192,1024]{3,2,1,0:T(8,128)(2,1)S(1)} %copy-done.3), channel_id=1, source_target_pairs={{0,4},{4,8},{8,12},{12,16},{16,20},{20,24},{24,28},{1,5},{5,9},{9,... | collective-permute-start | bytes 2359304 | tf_op jit(solution)/shard_map/ppermute | solution.py:199
  41.2 1.5 copy.28
  42.7 1.5 copy.29
  44.2 1.6 pad_maximum_fusion.1.refs_5_
  45.8 1.4 collective-permute-start.11
  47.2 4.3 %collective-permute-start.5 = (bf16[2,1,192,128]{3,2,1,0:T(8,128)(2,1)S(1)}, bf16[2,1,192,128]{3,2,1,0:T(8,128)(2,1)S(1)}, u32[]{:S(2)}, u32[]{:S(2)}) collective-permute-start(bf16[2,1,192,128]{3,2,1,0:T(8,128)(2,1)S(1)} %get-tuple-element.43), channel_id=1, source_target_pairs={{0,4},{4,8},{8,12},{12,16},{16,20},{20,24},{24,28},{1,5},{5,9},{9,... | collective-permute-start | bytes 294920 | tf_op jit(solution)/shard_map/ppermute | solution.py:211
  51.5 1.5 collective-permute-start.3
  53.0 30.1 %attend_row.4 = (bf16[2,4,192,1024]{3,2,1,0:T(8,128)(2,1)}, f32[8,128]{1,0:T(8,128)}) custom-call(bf16[2,1,192,1024]{3,2,1,0:T(8,128)(2,1)} %conv_row.4.refs_0_.refs_1_, bf16[2,1,192,1024]{3,2,1,0:T(8,128)(2,1)} %conv_row.4.refs_0_.refs_1_, bf16[2,1,192,1024]{3,2,1,0:T(8,128)(2,1)} %collective-permute-done.6.refs_2_, ...), custom_call_target="tpu_custom_call" | custom-call | flops 8589934592 | bytes 4718592 | tf_op jit(solution)/shard_map/attend_row/pallas_call | solution.py:157
  84.0 5.5 %conv_row.6.refs_0_.refs_1_ = bf16[2,1,192,1024]{3,2,1,0:T(8,128)(2,1)} custom-call(f32[4]{0:T(128)} %add_divide_fusion.side_ref, bf16[2,1,192,1024]{3,2,1,0:T(8,128)(2,1)} %copy-done.6, bf16[2,4,192,1024]{3,2,1,0:T(8,128)(2,1)} %xm.7, bf16[2,4,192,1024]{3,2,1,0:T(8,128)(2,1)} %xm.7, bf16[2,1,192,128]{3,2,1,0:T(8,128)(2,1)} %copy-done.10, ...), custom_call_target="tpu_custom_call" | custom-call | flops 1358954496 | bytes 3145728 | tf_op jit(solution)/shard_map/conv_row/pallas_call | solution.py:41
  90.2 5.5 %conv_row.7.refs_0_.refs_1_ = bf16[2,1,192,1024]{3,2,1,0:T(8,128)(2,1)} custom-call(f32[4]{0:T(128)} %add_divide_fusion.side_ref, bf16[2,4,192,1024]{3,2,1,0:T(8,128)(2,1)} %xm.7, bf16[2,4,192,1024]{3,2,1,0:T(8,128)(2,1)} %xm.7, bf16[2,1,192,1024]{3,2,1,0:T(8,128)(2,1)} %copy-done.7, bf16[2,4,192,128]{3,2,1,0:T(8,128)(2,1)} %pad_maximum_fusion.eu.em.ed, ...), custom_call_target="tpu_custom_call" | custom-call | flops 1358954496 | bytes 3145728 | tf_op jit(solution)/shard_map/conv_row/pallas_call | solution.py:41
  96.9 1.1 collective-permute-done.12.refs_3_
  98.0 1.1 collective-permute-done.13.refs_4_
  99.1 0.9 copy-done.18
  100.0 30.3 %attend_row.5 = (bf16[2,4,192,1024]{3,2,1,0:T(8,128)(2,1)}, f32[8,128]{1,0:T(8,128)}) custom-call(bf16[2,1,192,1024]{3,2,1,0:T(8,128)(2,1)} %conv_row.5.refs_0_.refs_1_, bf16[2,1,192,1024]{3,2,1,0:T(8,128)(2,1)} %conv_row.5.refs_0_.refs_1_, bf16[2,1,192,1024]{3,2,1,0:T(8,128)(2,1)} %copy-done.12, ...), custom_call_target="tpu_custom_call", output_to_operand_aliasing={{0}: (8, {})} | custom-call | flops 8589934592 | bytes 4718592 | tf_op jit(solution)/shard_map/attend_row/pallas_call | solution.py:157
  131.4 1.1 collective-permute-done.14.refs_3_
  132.6 1.1 collective-permute-done.15.refs_4_
  133.7 0.9 copy-done.19
  134.6 30.0 %attend_row.6 = (bf16[2,4,192,1024]{3,2,1,0:T(8,128)(2,1)}, f32[8,128]{1,0:T(8,128)}) custom-call(bf16[2,1,192,1024]{3,2,1,0:T(8,128)(2,1)} %conv_row.6.refs_0_.refs_1_, bf16[2,1,192,1024]{3,2,1,0:T(8,128)(2,1)} %conv_row.6.refs_0_.refs_1_, bf16[2,1,192,1024]{3,2,1,0:T(8,128)(2,1)} %copy-done.13, ...), custom_call_target="tpu_custom_call", output_to_operand_aliasing={{0}: (8, {})} | custom-call | flops 8589934592 | bytes 4718592 | tf_op jit(solution)/shard_map/attend_row/pallas_call | solution.py:157
  165.2 1.8 collective-permute-done.16.refs_3_
  167.0 1.1 collective-permute-done.17.refs_4_
  168.1 0.9 copy-done.20
  169.0 30.0 %attend_row.7 = (bf16[2,4,192,1024]{3,2,1,0:T(8,128)(2,1)}, f32[8,128]{1,0:T(8,128)}) custom-call(bf16[2,1,192,1024]{3,2,1,0:T(8,128)(2,1)} %conv_row.7.refs_0_.refs_1_, bf16[2,1,192,1024]{3,2,1,0:T(8,128)(2,1)} %conv_row.7.refs_0_.refs_1_, bf16[2,1,192,1024]{3,2,1,0:T(8,128)(2,1)} %copy-done.14, ...), custom_call_target="tpu_custom_call", output_to_operand_aliasing={{0}: (8, {})} | custom-call | flops 8589934592 | bytes 4718592 | tf_op jit(solution)/shard_map/attend_row/pallas_call | solution.py:157
  (67 shorter events, 6.5 us)
Async XLA Ops:
  1.6 7.1 %collective-permute-start.1 = (bf16[2,4,192]{2,1,0:T(4,128)(2,1)S(1)}, bf16[2,4,192]{2,1,0:T(4,128)(2,1)S(1)}, u32[]{:S(2)}, u32[]{:S(2)}) collective-permute-start(bf16[2,4,192]{2,1,0:T(4,128)(2,1)S(1)} %get-tuple-element.39), channel_id=1, source_target_pairs={{1,0},{2,1},{3,2},{0,3},{5,4},{6,5},{7,6},{4,7},{9,8},{10,9},{11,1... | collective-permute-start | bytes 9224 | tf_op jit(solution)/shard_map/ppermute | solution.py:202
  4.0 4.4 %collective-permute-start.2 = (bf16[2,4,192]{2,1,0:T(4,128)(2,1)S(1)}, bf16[2,4,192]{2,1,0:T(4,128)(2,1)S(1)}, u32[]{:S(2)}, u32[]{:S(2)}) collective-permute-start(bf16[2,4,192]{2,1,0:T(4,128)(2,1)S(1)} %get-tuple-element.40), channel_id=1, source_target_pairs={{0,1},{1,2},{2,3},{3,0},{4,5},{5,6},{6,7},{7,4},{8,9},{9,10},{10,1... | collective-permute-start | bytes 9224 | tf_op jit(solution)/shard_map/ppermute | solution.py:201
  6.5 3.6 %copy-start.4 = (bf16[2,1,192,1024]{3,2,1,0:T(8,128)(2,1)}, bf16[2,1,192,1024]{3,2,1,0:T(8,128)(2,1)S(1)}, u32[]{:S(2)}) copy-start(bf16[2,1,192,1024]{3,2,1,0:T(8,128)(2,1)S(1)} %get-tuple-element.22.refs_1_) | copy-start | bytes 2359300
  6.5 22.1 %collective-permute-start = (bf16[2,1,192,1024]{3,2,1,0:T(8,128)(2,1)S(1)}, bf16[2,1,192,1024]{3,2,1,0:T(8,128)(2,1)S(1)}, u32[]{:S(2)}, u32[]{:S(2)}) collective-permute-start(bf16[2,1,192,1024]{3,2,1,0:T(8,128)(2,1)S(1)} %get-tuple-element.22.refs_1_), channel_id=1, source_target_pairs={{4,0},{8,4},{12,8},{16,12},{20,16},{24,20},{28,24},{5,1},{9,5},{13... | collective-permute-start | bytes 2359304 | tf_op jit(solution)/shard_map/ppermute | solution.py:200
  15.5 13.0 %copy-start.2 = (bf16[2,1,192,1024]{3,2,1,0:T(8,128)(2,1)S(1)}, bf16[2,1,192,1024]{3,2,1,0:T(8,128)(2,1)}, u32[]{:S(2)}) copy-start(bf16[2,1,192,1024]{3,2,1,0:T(8,128)(2,1)} %conv_row.4.refs_0_.refs_1_) | copy-start | bytes 2359300
  15.5 20.6 %copy-start.3 = (bf16[2,1,192,1024]{3,2,1,0:T(8,128)(2,1)S(1)}, bf16[2,1,192,1024]{3,2,1,0:T(8,128)(2,1)}, u32[]{:S(2)}) copy-start(bf16[2,1,192,1024]{3,2,1,0:T(8,128)(2,1)} %get-tuple-element.23.refs_0_) | copy-start | bytes 2359300
  15.5 24.9 %copy-start.11 = (f32[128]{0:T(128)S(1)}, f32[128]{0:T(128)}, u32[]{:S(2)}) copy-start(f32[128]{0:T(128)} %param.10) | copy-start | bytes 1540
  15.5 31.7 %copy-start = (bf16[2,4,192,128]{3,2,1,0:T(8,128)(2,1)S(1)}, bf16[2,4,192,128]{3,2,1,0:T(8,128)(2,1)}, u32[]{:S(2)}) copy-start(bf16[2,4,192,128]{3,2,1,0:T(8,128)(2,1)} %pad_maximum_fusion.eu.em.ed) | copy-start | bytes 1179652
  15.6 20.6 %collective-permute-start.6 = (bf16[2,1,192,1024]{3,2,1,0:T(8,128)(2,1)}, bf16[2,1,192,1024]{3,2,1,0:T(8,128)(2,1)}, u32[]{:S(2)}, u32[]{:S(2)}) collective-permute-start(bf16[2,1,192,1024]{3,2,1,0:T(8,128)(2,1)} %conv_row.4.refs_0_.refs_1_), channel_id=1, source_target_pairs={{0,2},{1,3},{2,0},{3,1},{4,6},{5,7},{6,4},{7,5},{8,10},{9,11},{10,... | collective-permute-start | bytes 2359304 | tf_op jit(solution)/shard_map/ppermute | solution.py:235
  28.5 54.5 %copy-start.7 = (bf16[2,1,192,1024]{3,2,1,0:T(8,128)(2,1)}, bf16[2,1,192,1024]{3,2,1,0:T(8,128)(2,1)S(1)}, u32[]{:S(2)}) copy-start(bf16[2,1,192,1024]{3,2,1,0:T(8,128)(2,1)S(1)} %collective-permute-done.xd) | copy-start | bytes 2359300
  28.5 23.0 %collective-permute-start.7 = (bf16[2,1,192,1024]{3,2,1,0:T(8,128)(2,1)S(1)}, bf16[2,1,192,1024]{3,2,1,0:T(8,128)(2,1)}, u32[]{:S(2)}, u32[]{:S(2)}) collective-permute-start(bf16[2,1,192,1024]{3,2,1,0:T(8,128)(2,1)S(1)} %copy-done.2), channel_id=1, source_target_pairs={{0,1},{1,0},{2,3},{3,2},{4,5},{5,4},{6,7},{7,6},{8,9},{9,8},{10,11... | collective-permute-start | bytes 2359304 | tf_op jit(solution)/shard_map/ppermute | solution.py:238
  36.1 16.9 %collective-permute-start.8 = (bf16[2,1,192,1024]{3,2,1,0:T(8,128)(2,1)}, bf16[2,1,192,1024]{3,2,1,0:T(8,128)(2,1)}, u32[]{:S(2)}, u32[]{:S(2)}) collective-permute-start(bf16[2,1,192,1024]{3,2,1,0:T(8,128)(2,1)} %collective-permute-done.6.refs_2_), channel_id=1, source_target_pairs={{0,1},{1,0},{2,3},{3,2},{4,5},{5,4},{6,7},{7,6},{8,9},{9,8},{10,11... | collective-permute-start | bytes 2359304 | tf_op jit(solution)/shard_map/ppermute | solution.py:240
  36.1 47.0 %collective-permute-start.4 = (bf16[2,1,192,1024]{3,2,1,0:T(8,128)(2,1)S(1)}, bf16[2,1,192,1024]{3,2,1,0:T(8,128)(2,1)S(1)}, u32[]{:S(2)}, u32[]{:S(2)}) collective-permute-start(bf16[2,1,192,1024]{3,2,1,0:T(8,128)(2,1)S(1)} %copy-done.3), channel_id=1, source_target_pairs={{0,4},{4,8},{8,12},{12,16},{16,20},{20,24},{24,28},{1,5},{5,9},{9,... | collective-permute-start | bytes 2359304 | tf_op jit(solution)/shard_map/ppermute | solution.py:199
  45.8 49.8 %collective-permute-start.11 = (bf16[2,1,192,1024]{3,2,1,0:T(8,128)(2,1)}, bf16[2,1,192,1024]{3,2,1,0:T(8,128)(2,1)S(1)}, u32[]{:S(2)}, u32[]{:S(2)}) collective-permute-start(bf16[2,1,192,1024]{3,2,1,0:T(8,128)(2,1)} %conv_row.5.refs_0_.refs_1_), channel_id=1, source_target_pairs={{0,2},{1,3},{2,0},{3,1},{4,6},{5,7},{6,4},{7,5},{8,10},{9,11},{10,... | collective-permute-start | bytes 2359304 | tf_op jit(solution)/shard_map/ppermute | solution.py:235
  47.2 35.9 %collective-permute-start.5 = (bf16[2,1,192,128]{3,2,1,0:T(8,128)(2,1)S(1)}, bf16[2,1,192,128]{3,2,1,0:T(8,128)(2,1)S(1)}, u32[]{:S(2)}, u32[]{:S(2)}) collective-permute-start(bf16[2,1,192,128]{3,2,1,0:T(8,128)(2,1)S(1)} %get-tuple-element.43), channel_id=1, source_target_pairs={{0,4},{4,8},{8,12},{12,16},{16,20},{20,24},{24,28},{1,5},{5,9},{9,... | collective-permute-start | bytes 294920 | tf_op jit(solution)/shard_map/ppermute | solution.py:211
  51.5 38.0 %collective-permute-start.3 = (bf16[2,1,192,128]{3,2,1,0:T(8,128)(2,1)S(1)}, bf16[2,1,192,128]{3,2,1,0:T(8,128)(2,1)S(1)}, u32[]{:S(2)}, u32[]{:S(2)}) collective-permute-start(bf16[2,1,192,128]{3,2,1,0:T(8,128)(2,1)S(1)} %get-tuple-element.44), channel_id=1, source_target_pairs={{4,0},{8,4},{12,8},{16,12},{20,16},{24,20},{28,24},{5,1},{9,5},{13... | collective-permute-start | bytes 294920 | tf_op jit(solution)/shard_map/ppermute | solution.py:212
  89.5 6.1 %copy-start.5 = (bf16[2,1,192,1024]{3,2,1,0:T(8,128)(2,1)S(1)}, bf16[2,1,192,1024]{3,2,1,0:T(8,128)(2,1)}, u32[]{:S(2)}) copy-start(bf16[2,1,192,1024]{3,2,1,0:T(8,128)(2,1)} %conv_row.5.refs_0_.refs_1_) | copy-start | bytes 2359300
  89.5 6.7 %copy-start.1 = (bf16[2,1,192,1024]{3,2,1,0:T(8,128)(2,1)S(1)}, bf16[2,1,192,1024]{3,2,1,0:T(8,128)(2,1)}, u32[]{:S(2)}) copy-start(bf16[2,1,192,1024]{3,2,1,0:T(8,128)(2,1)} %conv_row.6.refs_0_.refs_1_) | copy-start | bytes 2359300
  95.7 3.5 %copy-start.12 = (bf16[2,1,192,1024]{3,2,1,0:T(8,128)(2,1)}, bf16[2,1,192,1024]{3,2,1,0:T(8,128)(2,1)S(1)}, u32[]{:S(2)}) copy-start(bf16[2,1,192,1024]{3,2,1,0:T(8,128)(2,1)S(1)} %collective-permute-done.11.refs_2_) | copy-start | bytes 2359300
  95.7 2.4 %collective-permute-start.12 = (bf16[2,1,192,1024]{3,2,1,0:T(8,128)(2,1)S(1)}, bf16[2,1,192,1024]{3,2,1,0:T(8,128)(2,1)S(1)}, u32[]{:S(2)}, u32[]{:S(2)}) collective-permute-start(bf16[2,1,192,1024]{3,2,1,0:T(8,128)(2,1)S(1)} %copy-done.5), channel_id=1, source_target_pairs={{0,1},{1,0},{2,3},{3,2},{4,5},{5,4},{6,7},{7,6},{8,9},{9,8},{10,11... | collective-permute-start | bytes 2359304 | tf_op jit(solution)/shard_map/ppermute | solution.py:238
  95.7 3.4 %collective-permute-start.13 = (bf16[2,1,192,1024]{3,2,1,0:T(8,128)(2,1)S(1)}, bf16[2,1,192,1024]{3,2,1,0:T(8,128)(2,1)S(1)}, u32[]{:S(2)}, u32[]{:S(2)}) collective-permute-start(bf16[2,1,192,1024]{3,2,1,0:T(8,128)(2,1)S(1)} %collective-permute-done.11.refs_2_), channel_id=1, source_target_pairs={{0,1},{1,0},{2,3},{3,2},{4,5},{5,4},{6,7},{7,6},{8,9},{9,8},{10,11... | collective-permute-start | bytes 2359304 | tf_op jit(solution)/shard_map/ppermute | solution.py:240
  96.2 34.2 %collective-permute-start.10 = (bf16[2,1,192,1024]{3,2,1,0:T(8,128)(2,1)S(1)}, bf16[2,1,192,1024]{3,2,1,0:T(8,128)(2,1)S(1)}, u32[]{:S(2)}, u32[]{:S(2)}) collective-permute-start(bf16[2,1,192,1024]{3,2,1,0:T(8,128)(2,1)S(1)} %copy-done.1), channel_id=1, source_target_pairs={{0,2},{1,3},{2,0},{3,1},{4,6},{5,7},{6,4},{7,5},{8,10},{9,11},{10,... | collective-permute-start | bytes 2359304 | tf_op jit(solution)/shard_map/ppermute | solution.py:235
  98.0 1.1 copy-start.16
  100.0 30.8 %copy-start.8 = (bf16[2,1,192,1024]{3,2,1,0:T(8,128)(2,1)S(1)}, bf16[2,1,192,1024]{3,2,1,0:T(8,128)(2,1)}, u32[]{:S(2)}) copy-start(bf16[2,1,192,1024]{3,2,1,0:T(8,128)(2,1)} %conv_row.7.refs_0_.refs_1_) | copy-start | bytes 2359300
  130.3 2.3 %collective-permute-start.14 = (bf16[2,1,192,1024]{3,2,1,0:T(8,128)(2,1)S(1)}, bf16[2,1,192,1024]{3,2,1,0:T(8,128)(2,1)S(1)}, u32[]{:S(2)}, u32[]{:S(2)}) collective-permute-start(bf16[2,1,192,1024]{3,2,1,0:T(8,128)(2,1)S(1)} %copy-done.1), channel_id=1, source_target_pairs={{0,1},{1,0},{2,3},{3,2},{4,5},{5,4},{6,7},{7,6},{8,9},{9,8},{10,11... | collective-permute-start | bytes 2359304 | tf_op jit(solution)/shard_map/ppermute | solution.py:238
  130.4 3.3 %copy-start.13 = (bf16[2,1,192,1024]{3,2,1,0:T(8,128)(2,1)}, bf16[2,1,192,1024]{3,2,1,0:T(8,128)(2,1)S(1)}, u32[]{:S(2)}) copy-start(bf16[2,1,192,1024]{3,2,1,0:T(8,128)(2,1)S(1)} %collective-permute-done.10.refs_2_) | copy-start | bytes 2359300
  130.4 3.3 %collective-permute-start.15 = (bf16[2,1,192,1024]{3,2,1,0:T(8,128)(2,1)S(1)}, bf16[2,1,192,1024]{3,2,1,0:T(8,128)(2,1)S(1)}, u32[]{:S(2)}, u32[]{:S(2)}) collective-permute-start(bf16[2,1,192,1024]{3,2,1,0:T(8,128)(2,1)S(1)} %collective-permute-done.10.refs_2_), channel_id=1, source_target_pairs={{0,1},{1,0},{2,3},{3,2},{4,5},{5,4},{6,7},{7,6},{8,9},{9,8},{10,11... | collective-permute-start | bytes 2359304 | tf_op jit(solution)/shard_map/ppermute | solution.py:240
  130.8 33.8 %collective-permute-start.9 = (bf16[2,1,192,1024]{3,2,1,0:T(8,128)(2,1)S(1)}, bf16[2,1,192,1024]{3,2,1,0:T(8,128)(2,1)S(1)}, u32[]{:S(2)}, u32[]{:S(2)}) collective-permute-start(bf16[2,1,192,1024]{3,2,1,0:T(8,128)(2,1)S(1)} %copy-done.8), channel_id=1, source_target_pairs={{0,2},{1,3},{2,0},{3,1},{4,6},{5,7},{6,4},{7,5},{8,10},{9,11},{10,... | collective-permute-start | bytes 2359304 | tf_op jit(solution)/shard_map/ppermute | solution.py:235
  132.6 1.1 copy-start.15
  164.6 3.5 %copy-start.14 = (bf16[2,1,192,1024]{3,2,1,0:T(8,128)(2,1)}, bf16[2,1,192,1024]{3,2,1,0:T(8,128)(2,1)S(1)}, u32[]{:S(2)}) copy-start(bf16[2,1,192,1024]{3,2,1,0:T(8,128)(2,1)S(1)} %collective-permute-done.9.refs_2_) | copy-start | bytes 2359300
  164.7 2.4 %collective-permute-start.16 = (bf16[2,1,192,1024]{3,2,1,0:T(8,128)(2,1)S(1)}, bf16[2,1,192,1024]{3,2,1,0:T(8,128)(2,1)S(1)}, u32[]{:S(2)}, u32[]{:S(2)}) collective-permute-start(bf16[2,1,192,1024]{3,2,1,0:T(8,128)(2,1)S(1)} %copy-done.8), channel_id=1, source_target_pairs={{0,1},{1,0},{2,3},{3,2},{4,5},{5,4},{6,7},{7,6},{8,9},{9,8},{10,11... | collective-permute-start | bytes 2359304 | tf_op jit(solution)/shard_map/ppermute | solution.py:238
  164.9 3.3 %collective-permute-start.17 = (bf16[2,1,192,1024]{3,2,1,0:T(8,128)(2,1)S(1)}, bf16[2,1,192,1024]{3,2,1,0:T(8,128)(2,1)S(1)}, u32[]{:S(2)}, u32[]{:S(2)}) collective-permute-start(bf16[2,1,192,1024]{3,2,1,0:T(8,128)(2,1)S(1)} %collective-permute-done.9.refs_2_), channel_id=1, source_target_pairs={{0,1},{1,0},{2,3},{3,2},{4,5},{5,4},{6,7},{7,6},{8,9},{9,8},{10,11... | collective-permute-start | bytes 2359304 | tf_op jit(solution)/shard_map/ppermute | solution.py:240
  (7 other events, 6.0 us)

commit v4 on v2

--- a/solution.py
+++ b/solution.py
@@ -62,7 +62,7 @@
     own = refs[0]
     blocks = refs[1 : 1 + count]
     wkv, gain, ow = refs[1 + count : 4 + count]
-    out_ref, token, kbuf, vbuf, qbuf, acc = refs[5 + count :]
+    out_ref, token, kbuf, vbuf, qbuf, acc = refs[-6:]
     chan = wkv.shape[0] // 2
     cols = own.shape[3]
     keys = kbuf.shape[0]
@@ -159,7 +159,8 @@
         grid=(2,),
         in_specs=[pl.BlockSpec((1, 1, chan, cols), lambda v: (v, 0, 0, 0))]
         + [pl.BlockSpec((1, 1, chan, cols), lambda v: (1 - v, 0, 0, 0))] * count
-        + [whole(wkv), whole(gain), whole(ow), pl.BlockSpec(memory_space=pl.ANY)],
+        + [whole(wkv), whole(gain), whole(ow)]
+        + [pl.BlockSpec(memory_space=pl.ANY) for _ in out_buf],
         out_specs=[
             pl.BlockSpec((1, 1, chan, cols), lambda v: (v, row, 0, 0)),
             pl.BlockSpec((8, 128), lambda v: (0, 0)),
@@ -174,7 +175,7 @@
             pltpu.VMEM((att, cols), BF16),
             pltpu.VMEM((att + 16, tj), F32),
         ],
-        input_output_aliases={4 + count: 0},
+        input_output_aliases={4 + count: 0} if out_buf else {},
         compiler_params=pltpu.CompilerParams(vmem_limit_bytes=VMEM_LIMIT),
         cost_estimate=pl.CostEstimate(
             flops=2 * 2 * 2 * 2 * cols * keys * att,
@@ -182,7 +183,7 @@
             transcendentals=2 * cols * keys,
         ),
         name="attend_row",
-    )(own, *blocks, wkv, gain, ow, out_buf)
+    )(own, *blocks, wkv, gain, ow, *out_buf)
 
 
 def body(views, conv_weight, match_weight, value_weight, post_gain, out_weight):
@@ -250,12 +251,13 @@
             after = lax.optimization_barrier((after[0], top, bottom))[:1]
         owns.append(convolve(r, after))
         after = (owns[-1],)
-    out = jnp.zeros(views.shape, BF16)
+    out = ()
     holds = [after, after]
     for i, (r, own) in enumerate(zip(order, owns)):
-        out, token = attend(out, (r, own, gather(own, holds[i])))
+        whole, token = attend(out, (r, own, gather(own, holds[i])))
+        out = (whole,)
         holds.append((token,))
-    return out
+    return out[0]
 
 
 def solution(mesh):

time: 194 us -> 195 us (level)
  the two profiles are of different devices: /device:TPU:0 before, /device:TPU:21 now
where the time goes in v4:
time: 195 us
  Pallas kernels  142 us (73%)
  starting transfers between devices  21.2 us (11%)
  waiting for transfers between devices  19 us (10%)
  local copies, waits for them, and re-layouts  9.48 us (5%)
  other arithmetic  2.24 us (1%)
    pallas_call x4, Pallas kernels, attend_row(): pl.pallas_call(functools.partial(attend_kernel, count, tj, tk), grid=(2,)...  120 us
    pallas_call x4, Pallas kernels, conv_row(): pl.pallas_call(functools.partial(conv_kernel, row), grid=(2,), in_specs=[...  22 us
    ppermute x1, waiting for transfers between devices, body(): bottom = lax.ppermute(first_row, 'lat', up)  12.1 us
    unnamed x44, local copies, waits for them, and re-layouts  4.99 us
    ppermute x1, starting transfers between devices, body(): top = lax.ppermute(last_row, 'lat', down)  4.05 us
    ppermute x4, starting transfers between devices, gather(): lax.ppermute(own, 'lon', [(i, (i + 2 * s) % lon) for i in range(lon)])  3.94 us
  transfers between devices with their start and end apart: 18, of which 4 were waited for; matrix products, arithmetic and copies ran while one was open for 3% of the time, Pallas kernels for 58%

profile of v4, /device:TPU:21, one launch (start us, length us, event | category | flops | bytes accessed | tf_op | source)
XLA Modules:
  0.0 194.6 jit_solution(11784802447827393582)
XLA Ops:
  0.0 1.6 slice_reduce_fusion.1
  1.6 0.7 collective-permute-start.1
  2.3 1.2 collective-permute-start.2
  3.5 1.5 fusion
  5.0 2.1 %collective-permute-start = (bf16[2,1,192,1024]{3,2,1,0:T(8,128)(2,1)S(1)}, bf16[2,1,192,1024]{3,2,1,0:T(8,128)(2,1)S(1)}, u32[]{:S(2)}, u32[]{:S(2)}) collective-permute-start(bf16[2,1,192,1024]{3,2,1,0:T(8,128)(2,1)S(1)} %get-tuple-element.22.refs_1_), channel_id=1, source_target_pairs={{4,0},{8,4},{12,8},{16,12},{20,16},{24,20},{28,24},{5,1},{9,5},{13... | collective-permute-start | bytes 2359304 | tf_op jit(solution)/shard_map/ppermute | solution.py:200
  7.2 4.0 %collective-permute-start.4 = (bf16[2,1,192,1024]{3,2,1,0:T(8,128)(2,1)S(1)}, bf16[2,1,192,1024]{3,2,1,0:T(8,128)(2,1)}, u32[]{:S(2)}, u32[]{:S(2)}) collective-permute-start(bf16[2,1,192,1024]{3,2,1,0:T(8,128)(2,1)S(1)} %get-tuple-element.23.refs_0_), channel_id=1, source_target_pairs={{0,4},{4,8},{8,12},{12,16},{16,20},{20,24},{24,28},{1,5},{5,9},{9,... | collective-permute-start | bytes 2359304 | tf_op jit(solution)/shard_map/ppermute | solution.py:199
  12.4 1.0 pad_maximum_fusion.eu.em.ed
  13.5 5.5 %conv_row.4.refs_0_.refs_1_ = bf16[2,1,192,1024]{3,2,1,0:T(8,128)(2,1)} custom-call(f32[4]{0:T(128)} %add_divide_fusion.side_ref, bf16[2,4,192,1024]{3,2,1,0:T(8,128)(2,1)} %xm.7, bf16[2,4,192,1024]{3,2,1,0:T(8,128)(2,1)} %xm.7, bf16[2,4,192,1024]{3,2,1,0:T(8,128)(2,1)} %xm.7, bf16[2,4,192,128]{3,2,1,0:T(8,128)(2,1)} %pad_maximum_fusion.eu.em.ed, ...), custom_call_target="tpu_custom_call" | custom-call | flops 1358954496 | bytes 3145728 | tf_op jit(solution)/shard_map/conv_row/pallas_call | solution.py:41
  19.0 1.1 collective-permute-start.10
  20.1 2.3 %collective-permute-start.5 = (bf16[2,1,192,128]{3,2,1,0:T(8,128)(2,1)S(1)}, bf16[2,1,192,128]{3,2,1,0:T(8,128)(2,1)S(1)}, u32[]{:S(2)}, u32[]{:S(2)}) collective-permute-start(bf16[2,1,192,128]{3,2,1,0:T(8,128)(2,1)S(1)} %get-tuple-element.43), channel_id=1, source_target_pairs={{0,4},{4,8},{8,12},{12,16},{16,20},{20,24},{24,28},{1,5},{5,9},{9,... | collective-permute-start | bytes 294920 | tf_op jit(solution)/shard_map/ppermute | solution.py:211
  22.4 3.2 %collective-permute-start.3 = (bf16[2,1,192,128]{3,2,1,0:T(8,128)(2,1)S(1)}, bf16[2,1,192,128]{3,2,1,0:T(8,128)(2,1)S(1)}, u32[]{:S(2)}, u32[]{:S(2)}) collective-permute-start(bf16[2,1,192,128]{3,2,1,0:T(8,128)(2,1)S(1)} %get-tuple-element.44), channel_id=1, source_target_pairs={{4,0},{8,4},{12,8},{16,12},{20,16},{24,20},{28,24},{5,1},{9,5},{13... | collective-permute-start | bytes 294920 | tf_op jit(solution)/shard_map/ppermute | solution.py:212
  25.6 5.5 %conv_row.5.refs_0_.refs_1_ = bf16[2,1,192,1024]{3,2,1,0:T(8,128)(2,1)} custom-call(f32[4]{0:T(128)} %add_divide_fusion.side_ref, bf16[2,4,192,1024]{3,2,1,0:T(8,128)(2,1)} %xm.7, bf16[2,4,192,1024]{3,2,1,0:T(8,128)(2,1)} %xm.7, bf16[2,4,192,1024]{3,2,1,0:T(8,128)(2,1)} %xm.7, bf16[2,4,192,128]{3,2,1,0:T(8,128)(2,1)} %pad_maximum_fusion.eu.em.ed, ...), custom_call_target="tpu_custom_call" | custom-call | flops 1358954496 | bytes 3145728 | tf_op jit(solution)/shard_map/conv_row/pallas_call | solution.py:41
  31.1 12.1 %collective-permute-done.xd = bf16[2,1,192,1024]{3,2,1,0:T(8,128)(2,1)S(1)} collective-permute-done((bf16[2,1,192,1024]{3,2,1,0:T(8,128)(2,1)S(1)}, bf16[2,1,192,1024]{3,2,1,0:T(8,128)(2,1)S(1)}, u32[]{:S(2)}, u32[]{:S(2)}) %collective-permute-start) | collective-permute-done | bytes 786464 | tf_op jit(solution)/shard_map/ppermute | solution.py:200
  43.2 1.4 collective-permute-start.7
  44.6 1.8 collective-permute-done.4.xu
  46.4 2.1 %collective-permute-done.5.eu = bf16[2,1,192,128]{3,2,1,0:T(8,128)(2,1)S(1)} collective-permute-done((bf16[2,1,192,128]{3,2,1,0:T(8,128)(2,1)S(1)}, bf16[2,1,192,128]{3,2,1,0:T(8,128)(2,1)S(1)}, u32[]{:S(2)}, u32[]{:S(2)}) %collective-permute-start.5) | collective-permute-done | bytes 98336 | tf_op jit(solution)/shard_map/ppermute | solution.py:211
  48.5 0.6 copy-done.9
  49.1 5.5 %conv_row.6.refs_0_.refs_1_ = bf16[2,1,192,1024]{3,2,1,0:T(8,128)(2,1)} custom-call(f32[4]{0:T(128)} %add_divide_fusion.side_ref, bf16[2,1,192,1024]{3,2,1,0:T(8,128)(2,1)} %collective-permute-done.4.xu, bf16[2,4,192,1024]{3,2,1,0:T(8,128)(2,1)} %xm.7, bf16[2,4,192,1024]{3,2,1,0:T(8,128)(2,1)} %xm.7, bf16[2,1,192,128]{3,2,1,0:T(8,128)(2,1)} %copy-done.9, ...), custom_call_target="tpu_custom_call" | custom-call | flops 1358954496 | bytes 3145728 | tf_op jit(solution)/shard_map/conv_row/pallas_call | solution.py:41
  55.3 5.5 %conv_row.7.refs_0_.refs_1_ = bf16[2,1,192,1024]{3,2,1,0:T(8,128)(2,1)} custom-call(f32[4]{0:T(128)} %add_divide_fusion.side_ref, bf16[2,4,192,1024]{3,2,1,0:T(8,128)(2,1)} %xm.7, bf16[2,4,192,1024]{3,2,1,0:T(8,128)(2,1)} %xm.7, bf16[2,1,192,1024]{3,2,1,0:T(8,128)(2,1)} %copy-done.7, bf16[2,4,192,128]{3,2,1,0:T(8,128)(2,1)} %pad_maximum_fusion.eu.em.ed, ...), custom_call_target="tpu_custom_call" | custom-call | flops 1358954496 | bytes 3145728 | tf_op jit(solution)/shard_map/conv_row/pallas_call | solution.py:41
  61.4 0.7 copy.31.refs_6_
  62.4 0.7 pad_maximum_fusion.1.refs_5_
  63.1 1.1 collective-permute-start.6
  64.6 0.9 collective-permute-start.8
  65.5 30.1 %attend_row.4 = (bf16[2,4,192,1024]{3,2,1,0:T(8,128)(2,1)}, f32[8,128]{1,0:T(8,128)}) custom-call(bf16[2,1,192,1024]{3,2,1,0:T(8,128)(2,1)} %conv_row.4.refs_0_.refs_1_, bf16[2,1,192,1024]{3,2,1,0:T(8,128)(2,1)} %conv_row.4.refs_0_.refs_1_, bf16[2,1,192,1024]{3,2,1,0:T(8,128)(2,1)} %collective-permute-done.10.refs_2_, ...), custom_call_target="tpu_custom_call" | custom-call | flops 8589934592 | bytes 4718592 | tf_op jit(solution)/shard_map/attend_row/pallas_call | solution.py:157
  96.0 2.9 %collective-permute-done.15.refs_2_ = bf16[2,1,192,1024]{3,2,1,0:T(8,128)(2,1)S(1)} collective-permute-done((bf16[2,1,192,1024]{3,2,1,0:T(8,128)(2,1)S(1)}, bf16[2,1,192,1024]{3,2,1,0:T(8,128)(2,1)S(1)}, u32[]{:S(2)}, u32[]{:S(2)}) %collective-permute-start.15) | collective-permute-done | bytes 786464 | tf_op jit(solution)/shard_map/ppermute | solution.py:235
  98.9 1.2 collective-permute-start.17
  100.1 0.9 copy-done.16
  101.3 30.3 %attend_row.5 = (bf16[2,4,192,1024]{3,2,1,0:T(8,128)(2,1)}, f32[8,128]{1,0:T(8,128)}) custom-call(bf16[2,1,192,1024]{3,2,1,0:T(8,128)(2,1)} %conv_row.5.refs_0_.refs_1_, bf16[2,1,192,1024]{3,2,1,0:T(8,128)(2,1)} %conv_row.5.refs_0_.refs_1_, bf16[2,1,192,1024]{3,2,1,0:T(8,128)(2,1)} %collective-permute-done.7.refs_2_, ...), custom_call_target="tpu_custom_call", output_to_operand_aliasing={{0}: (8, {})} | custom-call | flops 8589934592 | bytes 4718592 | tf_op jit(solution)/shard_map/attend_row/pallas_call | solution.py:157
  132.2 0.9 copy-done.15
  133.3 30.0 %attend_row.6 = (bf16[2,4,192,1024]{3,2,1,0:T(8,128)(2,1)}, f32[8,128]{1,0:T(8,128)}) custom-call(bf16[2,1,192,1024]{3,2,1,0:T(8,128)(2,1)} %conv_row.6.refs_0_.refs_1_, bf16[2,1,192,1024]{3,2,1,0:T(8,128)(2,1)} %conv_row.6.refs_0_.refs_1_, bf16[2,1,192,1024]{3,2,1,0:T(8,128)(2,1)} %copy-done.14, ...), custom_call_target="tpu_custom_call", output_to_operand_aliasing={{0}: (8, {})} | custom-call | flops 8589934592 | bytes 4718592 | tf_op jit(solution)/shard_map/attend_row/pallas_call | solution.py:157
  163.4 0.9 copy-done.18
  164.5 30.1 %attend_row.7 = (bf16[2,4,192,1024]{3,2,1,0:T(8,128)(2,1)}, f32[8,128]{1,0:T(8,128)}) custom-call(bf16[2,1,192,1024]{3,2,1,0:T(8,128)(2,1)} %conv_row.7.refs_0_.refs_1_, bf16[2,1,192,1024]{3,2,1,0:T(8,128)(2,1)} %conv_row.7.refs_0_.refs_1_, bf16[2,1,192,1024]{3,2,1,0:T(8,128)(2,1)} %copy-done.13, ...), custom_call_target="tpu_custom_call", output_to_operand_aliasing={{0}: (8, {})} | custom-call | flops 8589934592 | bytes 4718592 | tf_op jit(solution)/shard_map/attend_row/pallas_call | solution.py:157
  (67 shorter events, 5.1 us)
Async XLA Ops:
  1.6 10.5 %collective-permute-start.1 = (bf16[2,4,192]{2,1,0:T(4,128)(2,1)S(1)}, bf16[2,4,192]{2,1,0:T(4,128)(2,1)S(1)}, u32[]{:S(2)}, u32[]{:S(2)}) collective-permute-start(bf16[2,4,192]{2,1,0:T(4,128)(2,1)S(1)} %get-tuple-element.39), channel_id=1, source_target_pairs={{1,0},{2,1},{3,2},{0,3},{5,4},{6,5},{7,6},{4,7},{9,8},{10,9},{11,1... | collective-permute-start | bytes 9224 | tf_op jit(solution)/shard_map/ppermute | solution.py:202
  2.3 9.5 %collective-permute-start.2 = (bf16[2,4,192]{2,1,0:T(4,128)(2,1)S(1)}, bf16[2,4,192]{2,1,0:T(4,128)(2,1)S(1)}, u32[]{:S(2)}, u32[]{:S(2)}) collective-permute-start(bf16[2,4,192]{2,1,0:T(4,128)(2,1)S(1)} %get-tuple-element.40), channel_id=1, source_target_pairs={{0,1},{1,2},{2,3},{3,0},{4,5},{5,6},{6,7},{7,4},{8,9},{9,10},{10,1... | collective-permute-start | bytes 9224 | tf_op jit(solution)/shard_map/ppermute | solution.py:201
  5.0 8.5 %copy-start.3 = (bf16[2,1,192,1024]{3,2,1,0:T(8,128)(2,1)}, bf16[2,1,192,1024]{3,2,1,0:T(8,128)(2,1)S(1)}, u32[]{:S(2)}) copy-start(bf16[2,1,192,1024]{3,2,1,0:T(8,128)(2,1)S(1)} %get-tuple-element.23.refs_0_) | copy-start | bytes 2359300
  5.0 8.5 %copy-start.4 = (bf16[2,1,192,1024]{3,2,1,0:T(8,128)(2,1)}, bf16[2,1,192,1024]{3,2,1,0:T(8,128)(2,1)S(1)}, u32[]{:S(2)}) copy-start(bf16[2,1,192,1024]{3,2,1,0:T(8,128)(2,1)S(1)} %get-tuple-element.22.refs_1_) | copy-start | bytes 2359300
  5.0 38.2 %collective-permute-start = (bf16[2,1,192,1024]{3,2,1,0:T(8,128)(2,1)S(1)}, bf16[2,1,192,1024]{3,2,1,0:T(8,128)(2,1)S(1)}, u32[]{:S(2)}, u32[]{:S(2)}) collective-permute-start(bf16[2,1,192,1024]{3,2,1,0:T(8,128)(2,1)S(1)} %get-tuple-element.22.refs_1_), channel_id=1, source_target_pairs={{4,0},{8,4},{12,8},{16,12},{20,16},{24,20},{28,24},{5,1},{9,5},{13... | collective-permute-start | bytes 2359304 | tf_op jit(solution)/shard_map/ppermute | solution.py:200
  7.2 39.2 %collective-permute-start.4 = (bf16[2,1,192,1024]{3,2,1,0:T(8,128)(2,1)S(1)}, bf16[2,1,192,1024]{3,2,1,0:T(8,128)(2,1)}, u32[]{:S(2)}, u32[]{:S(2)}) collective-permute-start(bf16[2,1,192,1024]{3,2,1,0:T(8,128)(2,1)S(1)} %get-tuple-element.23.refs_0_), channel_id=1, source_target_pairs={{0,4},{4,8},{8,12},{12,16},{16,20},{20,24},{24,28},{1,5},{5,9},{9,... | collective-permute-start | bytes 2359304 | tf_op jit(solution)/shard_map/ppermute | solution.py:199
  13.5 6.6 %copy-start = (bf16[2,4,192,128]{3,2,1,0:T(8,128)(2,1)S(1)}, bf16[2,4,192,128]{3,2,1,0:T(8,128)(2,1)}, u32[]{:S(2)}) copy-start(bf16[2,4,192,128]{3,2,1,0:T(8,128)(2,1)} %pad_maximum_fusion.eu.em.ed) | copy-start | bytes 1179652
  19.0 42.3 %collective-permute-start.10 = (bf16[2,1,192,1024]{3,2,1,0:T(8,128)(2,1)}, bf16[2,1,192,1024]{3,2,1,0:T(8,128)(2,1)}, u32[]{:S(2)}, u32[]{:S(2)}) collective-permute-start(bf16[2,1,192,1024]{3,2,1,0:T(8,128)(2,1)} %conv_row.4.refs_0_.refs_1_), channel_id=1, source_target_pairs={{0,2},{1,3},{2,0},{3,1},{4,6},{5,7},{6,4},{7,5},{8,10},{9,11},{10,... | collective-permute-start | bytes 2359304 | tf_op jit(solution)/shard_map/ppermute | solution.py:235
  20.1 28.4 %collective-permute-start.5 = (bf16[2,1,192,128]{3,2,1,0:T(8,128)(2,1)S(1)}, bf16[2,1,192,128]{3,2,1,0:T(8,128)(2,1)S(1)}, u32[]{:S(2)}, u32[]{:S(2)}) collective-permute-start(bf16[2,1,192,128]{3,2,1,0:T(8,128)(2,1)S(1)} %get-tuple-element.43), channel_id=1, source_target_pairs={{0,4},{4,8},{8,12},{12,16},{16,20},{20,24},{24,28},{1,5},{5,9},{9,... | collective-permute-start | bytes 294920 | tf_op jit(solution)/shard_map/ppermute | solution.py:211
  22.4 32.3 %collective-permute-start.3 = (bf16[2,1,192,128]{3,2,1,0:T(8,128)(2,1)S(1)}, bf16[2,1,192,128]{3,2,1,0:T(8,128)(2,1)S(1)}, u32[]{:S(2)}, u32[]{:S(2)}) collective-permute-start(bf16[2,1,192,128]{3,2,1,0:T(8,128)(2,1)S(1)} %get-tuple-element.44), channel_id=1, source_target_pairs={{4,0},{8,4},{12,8},{16,12},{20,16},{24,20},{28,24},{5,1},{9,5},{13... | collective-permute-start | bytes 294920 | tf_op jit(solution)/shard_map/ppermute | solution.py:212
  43.2 11.4 %copy-start.7 = (bf16[2,1,192,1024]{3,2,1,0:T(8,128)(2,1)}, bf16[2,1,192,1024]{3,2,1,0:T(8,128)(2,1)S(1)}, u32[]{:S(2)}) copy-start(bf16[2,1,192,1024]{3,2,1,0:T(8,128)(2,1)S(1)} %collective-permute-done.xd) | copy-start | bytes 2359300
  43.2 21.3 %collective-permute-start.7 = (bf16[2,1,192,1024]{3,2,1,0:T(8,128)(2,1)}, bf16[2,1,192,1024]{3,2,1,0:T(8,128)(2,1)}, u32[]{:S(2)}, u32[]{:S(2)}) collective-permute-start(bf16[2,1,192,1024]{3,2,1,0:T(8,128)(2,1)} %conv_row.5.refs_0_.refs_1_), channel_id=1, source_target_pairs={{0,2},{1,3},{2,0},{3,1},{4,6},{5,7},{6,4},{7,5},{8,10},{9,11},{10,... | collective-permute-start | bytes 2359304 | tf_op jit(solution)/shard_map/ppermute | solution.py:235
  54.6 6.2 %copy-start.2 = (bf16[2,1,192,1024]{3,2,1,0:T(8,128)(2,1)S(1)}, bf16[2,1,192,1024]{3,2,1,0:T(8,128)(2,1)}, u32[]{:S(2)}) copy-start(bf16[2,1,192,1024]{3,2,1,0:T(8,128)(2,1)} %conv_row.4.refs_0_.refs_1_) | copy-start | bytes 2359300
  54.6 6.8 %copy-start.12 = (f32[128]{0:T(128)S(1)}, f32[128]{0:T(128)}, u32[]{:S(2)}) copy-start(f32[128]{0:T(128)} %param.10) | copy-start | bytes 1540
  54.6 7.5 %copy-start.10 = (bf16[128,192]{0,1:T(8,128)(2,1)S(1)}, bf16[128,192]{0,1:T(8,128)(2,1)}, u32[]{:S(2)}) copy-start(bf16[128,192]{0,1:T(8,128)(2,1)} %param.8) | copy-start | bytes 147460
  54.6 7.6 %copy-start.11 = (bf16[128,192]{0,1:T(8,128)(2,1)S(1)}, bf16[128,192]{0,1:T(8,128)(2,1)}, u32[]{:S(2)}) copy-start(bf16[128,192]{0,1:T(8,128)(2,1)} %param.9) | copy-start | bytes 147460
  54.7 9.5 %copy-start.5 = (bf16[2,1,192,1024]{3,2,1,0:T(8,128)(2,1)S(1)}, bf16[2,1,192,1024]{3,2,1,0:T(8,128)(2,1)}, u32[]{:S(2)}) copy-start(bf16[2,1,192,1024]{3,2,1,0:T(8,128)(2,1)} %conv_row.6.refs_0_.refs_1_) | copy-start | bytes 2359300
  54.7 9.9 %copy-start.1 = (bf16[2,1,192,1024]{3,2,1,0:T(8,128)(2,1)S(1)}, bf16[2,1,192,1024]{3,2,1,0:T(8,128)(2,1)}, u32[]{:S(2)}) copy-start(bf16[2,1,192,1024]{3,2,1,0:T(8,128)(2,1)} %conv_row.5.refs_0_.refs_1_) | copy-start | bytes 2359300
  60.9 4.6 %collective-permute-start.11 = (bf16[2,1,192,1024]{3,2,1,0:T(8,128)(2,1)S(1)}, bf16[2,1,192,1024]{3,2,1,0:T(8,128)(2,1)}, u32[]{:S(2)}, u32[]{:S(2)}) collective-permute-start(bf16[2,1,192,1024]{3,2,1,0:T(8,128)(2,1)S(1)} %copy-done.2), channel_id=1, source_target_pairs={{0,1},{1,0},{2,3},{3,2},{4,5},{5,4},{6,7},{7,6},{8,9},{9,8},{10,11... | collective-permute-start | bytes 2359304 | tf_op jit(solution)/shard_map/ppermute | solution.py:238
  61.3 4.3 %collective-permute-start.12 = (bf16[2,1,192,1024]{3,2,1,0:T(8,128)(2,1)}, bf16[2,1,192,1024]{3,2,1,0:T(8,128)(2,1)}, u32[]{:S(2)}, u32[]{:S(2)}) collective-permute-start(bf16[2,1,192,1024]{3,2,1,0:T(8,128)(2,1)} %collective-permute-done.10.refs_2_), channel_id=1, source_target_pairs={{0,1},{1,0},{2,3},{3,2},{4,5},{5,4},{6,7},{7,6},{8,9},{9,8},{10,11... | collective-permute-start | bytes 2359304 | tf_op jit(solution)/shard_map/ppermute | solution.py:240
  63.1 68.6 %collective-permute-start.6 = (bf16[2,1,192,1024]{3,2,1,0:T(8,128)(2,1)}, bf16[2,1,192,1024]{3,2,1,0:T(8,128)(2,1)S(1)}, u32[]{:S(2)}, u32[]{:S(2)}) collective-permute-start(bf16[2,1,192,1024]{3,2,1,0:T(8,128)(2,1)} %conv_row.7.refs_0_.refs_1_), channel_id=1, source_target_pairs={{0,2},{1,3},{2,0},{3,1},{4,6},{5,7},{6,4},{7,5},{8,10},{9,11},{10,... | collective-permute-start | bytes 2359304 | tf_op jit(solution)/shard_map/ppermute | solution.py:235
  64.1 34.8 %collective-permute-start.15 = (bf16[2,1,192,1024]{3,2,1,0:T(8,128)(2,1)S(1)}, bf16[2,1,192,1024]{3,2,1,0:T(8,128)(2,1)S(1)}, u32[]{:S(2)}, u32[]{:S(2)}) collective-permute-start(bf16[2,1,192,1024]{3,2,1,0:T(8,128)(2,1)S(1)} %copy-done.5), channel_id=1, source_target_pairs={{0,2},{1,3},{2,0},{3,1},{4,6},{5,7},{6,4},{7,5},{8,10},{9,11},{10,... | collective-permute-start | bytes 2359304 | tf_op jit(solution)/shard_map/ppermute | solution.py:235
  64.6 35.6 %collective-permute-start.8 = (bf16[2,1,192,1024]{3,2,1,0:T(8,128)(2,1)S(1)}, bf16[2,1,192,1024]{3,2,1,0:T(8,128)(2,1)S(1)}, u32[]{:S(2)}, u32[]{:S(2)}) collective-permute-start(bf16[2,1,192,1024]{3,2,1,0:T(8,128)(2,1)S(1)} %copy-done.1), channel_id=1, source_target_pairs={{0,1},{1,0},{2,3},{3,2},{4,5},{5,4},{6,7},{7,6},{8,9},{9,8},{10,11... | collective-permute-start | bytes 2359304 | tf_op jit(solution)/shard_map/ppermute | solution.py:238
  65.5 34.7 %collective-permute-start.9 = (bf16[2,1,192,1024]{3,2,1,0:T(8,128)(2,1)}, bf16[2,1,192,1024]{3,2,1,0:T(8,128)(2,1)S(1)}, u32[]{:S(2)}, u32[]{:S(2)}) collective-permute-start(bf16[2,1,192,1024]{3,2,1,0:T(8,128)(2,1)} %collective-permute-done.7.refs_2_), channel_id=1, source_target_pairs={{0,1},{1,0},{2,3},{3,2},{4,5},{5,4},{6,7},{7,6},{8,9},{9,8},{10,11... | collective-permute-start | bytes 2359304 | tf_op jit(solution)/shard_map/ppermute | solution.py:240
  95.6 36.6 %collective-permute-start.16 = (bf16[2,1,192,1024]{3,2,1,0:T(8,128)(2,1)S(1)}, bf16[2,1,192,1024]{3,2,1,0:T(8,128)(2,1)S(1)}, u32[]{:S(2)}, u32[]{:S(2)}) collective-permute-start(bf16[2,1,192,1024]{3,2,1,0:T(8,128)(2,1)S(1)} %copy-done.5), channel_id=1, source_target_pairs={{0,1},{1,0},{2,3},{3,2},{4,5},{5,4},{6,7},{7,6},{8,9},{9,8},{10,11... | collective-permute-start | bytes 2359304 | tf_op jit(solution)/shard_map/ppermute | solution.py:238
  98.9 32.6 %copy-start.14 = (bf16[2,1,192,1024]{3,2,1,0:T(8,128)(2,1)}, bf16[2,1,192,1024]{3,2,1,0:T(8,128)(2,1)S(1)}, u32[]{:S(2)}) copy-start(bf16[2,1,192,1024]{3,2,1,0:T(8,128)(2,1)S(1)} %collective-permute-done.15.refs_2_) | copy-start | bytes 2359300
  98.9 33.2 %collective-permute-start.17 = (bf16[2,1,192,1024]{3,2,1,0:T(8,128)(2,1)S(1)}, bf16[2,1,192,1024]{3,2,1,0:T(8,128)(2,1)S(1)}, u32[]{:S(2)}, u32[]{:S(2)}) collective-permute-start(bf16[2,1,192,1024]{3,2,1,0:T(8,128)(2,1)S(1)} %collective-permute-done.15.refs_2_), channel_id=1, source_target_pairs={{0,1},{1,0},{2,3},{3,2},{4,5},{5,4},{6,7},{7,6},{8,9},{9,8},{10,11... | collective-permute-start | bytes 2359304 | tf_op jit(solution)/shard_map/ppermute | solution.py:240
  100.1 1.2 copy-start.19
  101.3 30.3 %copy-start.6 = (bf16[2,1,192,1024]{3,2,1,0:T(8,128)(2,1)S(1)}, bf16[2,1,192,1024]{3,2,1,0:T(8,128)(2,1)}, u32[]{:S(2)}) copy-start(bf16[2,1,192,1024]{3,2,1,0:T(8,128)(2,1)} %conv_row.7.refs_0_.refs_1_) | copy-start | bytes 2359300
  131.6 31.8 %collective-permute-start.13 = (bf16[2,1,192,1024]{3,2,1,0:T(8,128)(2,1)S(1)}, bf16[2,1,192,1024]{3,2,1,0:T(8,128)(2,1)S(1)}, u32[]{:S(2)}, u32[]{:S(2)}) collective-permute-start(bf16[2,1,192,1024]{3,2,1,0:T(8,128)(2,1)S(1)} %copy-done.6), channel_id=1, source_target_pairs={{0,1},{1,0},{2,3},{3,2},{4,5},{5,4},{6,7},{7,6},{8,9},{9,8},{10,11... | collective-permute-start | bytes 2359304 | tf_op jit(solution)/shard_map/ppermute | solution.py:238
  131.7 31.7 %copy-start.13 = (bf16[2,1,192,1024]{3,2,1,0:T(8,128)(2,1)}, bf16[2,1,192,1024]{3,2,1,0:T(8,128)(2,1)S(1)}, u32[]{:S(2)}) copy-start(bf16[2,1,192,1024]{3,2,1,0:T(8,128)(2,1)S(1)} %collective-permute-done.6.refs_2_) | copy-start | bytes 2359300
  131.7 31.7 %collective-permute-start.14 = (bf16[2,1,192,1024]{3,2,1,0:T(8,128)(2,1)S(1)}, bf16[2,1,192,1024]{3,2,1,0:T(8,128)(2,1)S(1)}, u32[]{:S(2)}, u32[]{:S(2)}) collective-permute-start(bf16[2,1,192,1024]{3,2,1,0:T(8,128)(2,1)S(1)} %collective-permute-done.6.refs_2_), channel_id=1, source_target_pairs={{0,1},{1,0},{2,3},{3,2},{4,5},{5,4},{6,7},{7,6},{8,9},{9,8},{10,11... | collective-permute-start | bytes 2359304 | tf_op jit(solution)/shard_map/ppermute | solution.py:240
  (7 other events, 6.3 us)
